TPU v7x, 256 devices: a whole 4x4x8 slice. The times are simulated.
256 devices in a mesh: lat: 16 (over y, x_lo, core), lon: 16 (over x_hi, z).
Axes of the slice: x: 4 (x_hi: 2, x_lo: 2; x = x_hi * 2 + x_lo), y: 4, z: 8, core: 2. Of those that a mesh axis runs over, the one named last changes fastest.
Arguments:
- state: bfloat16 [256, 384, 2048], P(None, 'lat', 'lon'), may hold values from -6 to 6
- obs_values: bfloat16 [64, 524288], P(None, ('lat', 'lon')), may hold values from -6 to 6
- obs_offsets: float32 [2, 524288], P(None, ('lat', 'lon')), may hold values from 0 to 1
- obs_cell: int32 [524288], P(('lat', 'lon')), may hold values from 0 to 3071, as said below
- obs_count: int32 [256], P(('lat', 'lon')), may hold values from 64 to 2048, as said below
- w_in: bfloat16 [65, 256], replicated, may hold values from -0.75 to 0.75
- dw_weight: float32 [256, 7, 7], replicated, may hold values from -0.875 to 0.875
- dw_bias: float32 [256], replicated, may hold values from -3 to 3
- norm_gain: float32 [256], replicated, may hold values from 0.1 to 1.9
- norm_bias: float32 [256], replicated, may hold values from -3 to 3
- w_up: bfloat16 [256, 1024], replicated, may hold values from -0.375 to 0.375
- up_bias: float32 [1024], replicated, may hold values from -3 to 3
- w_down: bfloat16 [1024, 256], replicated, may hold values from -0.1875 to 0.1875
- down_bias: float32 [256], replicated, may hold values from -3 to 3
- layer_scale: float32 [256], replicated, may hold values from 0.1 to 1.9
Outputs:
- result: bfloat16 [256, 384, 2048], P(None, 'lat', 'lon')
Inputs may be any that keep to these rules, and one draw needn't show every extreme that they name: obs_cell numbers a cell inside the slot's own tile as row * 128 + column, row below 24 and column below 128, padding slots included; tiles are numbered along latitude first, then longitude, tile t holding latitude rows from 24 * (t // 16) and longitude columns from 128 * (t % 16). The live slots of each tile are its first obs_count slots; the rest are padding.
All inputs are finite; a program needn't handle non-finite values.
Results may differ from a plain program's by a relative error of at most 0.0065.
Values may be sent and summed in bfloat16 or wider, within the bound.
No kernel may reach another device: no remote copies, remote signals or barrier semaphores. Data moves between devices by JAX's collectives and lax.ppermute only.
A program may use at most 128 MiB of HBM per device.

v0:
```python
import jax
import jax.numpy as jnp
from jax import lax
from jax.sharding import PartitionSpec as P

KERNEL = 7
W = 4
BLOCK = 128


inverse_width = 1.0 / (2.0 * 1.5 * 1.5)


def with_halo(x, sides, width, wrap):
    for axis, dim in sides:
        size, length = (lax.axis_size(axis), x.shape[dim])
        up = [(i, (i + 1) % size) for i in range(size if wrap else size - 1)]
        down = [(j, i) for i, j in up]
        last = lax.slice_in_dim(x, length - width, length, axis=dim)
        initial = lax.slice_in_dim(x, 0, width, axis=dim)
        before = lax.ppermute(last, axis, up)
        after = lax.ppermute(initial, axis, down)
        x = jnp.concatenate([before, x, after], axis=dim)
    return x


def gaussian_rows(offset, cell_index, extent, base, live_rows):
    places = lax.broadcasted_iota(jnp.int32, (extent, cell_index.shape[0]), 0) - base
    apart = places - cell_index[None, :]
    inside = (jnp.abs(apart) <= W) & live_rows[None, :]
    spread = offset[None, :] - apart.astype(jnp.float32) - 0.5
    return jnp.where(inside, jnp.exp(-spread * spread * inverse_width), 0.0)


def accumulate(packed, live_count, ext_rows, ext_cols, base):
    channels_in = packed.shape[0] - 5
    live_blocks = (live_count + BLOCK - 1) // BLOCK

    def add_block(number, running):
        weighted, density = running
        row_start = number * BLOCK
        piece = lax.dynamic_slice_in_dim(packed, row_start, BLOCK, 1)
        values = piece[:channels_in]
        lat_cells = piece[channels_in + 2].astype(jnp.int32)
        lon_cells = piece[channels_in + 3].astype(jnp.int32)
        live_rows = row_start + lax.iota(jnp.int32, BLOCK) < live_count
        lat_weight = gaussian_rows(piece[channels_in], lat_cells, ext_rows, base, live_rows)
        lon_weight = gaussian_rows(piece[channels_in + 1], lon_cells, ext_cols, base, live_rows)
        scaled = (values[:, None, :] * lat_weight[None, :, :]).astype(jnp.bfloat16)
        scaled = scaled.reshape(channels_in * ext_rows, BLOCK)
        contract = (((1,), (1,)), ((), ()))
        weighted = weighted + lax.dot_general(
            scaled, lon_weight.astype(jnp.bfloat16), contract, preferred_element_type=jnp.float32
        )
        density = density + lax.dot_general(
            lat_weight,
            lon_weight,
            contract,
            precision=lax.Precision.HIGHEST,
            preferred_element_type=jnp.float32,
        )
        return (weighted, density)

    start_weighted = jnp.zeros((channels_in * ext_rows, ext_cols), jnp.float32)
    start_density = jnp.zeros((ext_rows, ext_cols), jnp.float32)
    weighted, density = lax.fori_loop(0, live_blocks, add_block, (start_weighted, start_density))
    return jnp.concatenate(
        [weighted.reshape(channels_in, ext_rows, ext_cols), density[None, :, :]], 0
    )


def observation_sums(obs_values, obs_offsets, obs_cell, obs_count, rows_tile, cols_tile):
    slots = obs_cell.shape[0]
    live_count = obs_count[0]
    live_flag = (lax.iota(jnp.int32, slots) < live_count).astype(jnp.float32)
    own_rows = jnp.concatenate(
        [
            obs_values.astype(jnp.float32),
            obs_offsets,
            (obs_cell // cols_tile).astype(jnp.float32)[None, :],
            (obs_cell % cols_tile).astype(jnp.float32)[None, :],
            live_flag[None, :],
        ],
        0,
    )
    ext_rows = rows_tile + 2 * W
    ext_cols = cols_tile + 2 * W
    partial_value = accumulate(own_rows, live_count, ext_rows, ext_cols, W)
    beside = with_halo(partial_value.astype(jnp.bfloat16), (("lon", 2),), W, True).astype(
        partial_value.dtype
    )
    folded = jnp.concatenate(
        [
            partial_value[:, :, W : 2 * W] + beside[:, :, :W],
            partial_value[:, :, 2 * W : cols_tile],
            partial_value[:, :, cols_tile : cols_tile + W] + beside[:, :, ext_cols + W :],
        ],
        2,
    )
    lat_rims = with_halo(folded.astype(jnp.bfloat16), (("lat", 1),), W, False).astype(folded.dtype)
    gathered = jnp.concatenate(
        [
            folded[:, W : 2 * W, :] + lat_rims[:, :W, :],
            folded[:, 2 * W : rows_tile, :],
            folded[:, rows_tile : rows_tile + W, :] + lat_rims[:, ext_rows + W :, :],
        ],
        1,
    )
    return gathered.astype(jnp.bfloat16)


def encode(sources, state, w_in):
    projected = jnp.einsum("spq,sc->cpq", sources, w_in, preferred_element_type=jnp.float32)
    return (state.astype(jnp.float32) + projected).astype(jnp.bfloat16)


def local(
    state,
    obs_values,
    obs_offsets,
    obs_cell,
    obs_count,
    w_in,
    dw_weight,
    dw_bias,
    norm_gain,
    norm_bias,
    w_up,
    up_bias,
    w_down,
    down_bias,
    layer_scale,
):
    channels, rows_tile, cols_tile = state.shape
    margin = KERNEL // 2
    sources = observation_sums(obs_values, obs_offsets, obs_cell, obs_count, rows_tile, cols_tile)
    mixed = encode(sources, state, w_in)
    mixed_wide = with_halo(mixed, (("lon", 2),), margin, True)
    padded = with_halo(mixed_wide, (("lat", 1),), margin, False)
    filtered = jnp.zeros((channels, rows_tile, cols_tile), jnp.float32) + dw_bias[:, None, None]
    for shift_row in range(KERNEL):
        for shift_col in range(KERNEL):
            window = padded[:, shift_row : shift_row + rows_tile, shift_col : shift_col + cols_tile]
            filtered = (
                filtered
                + window.astype(jnp.float32) * dw_weight[:, shift_row, shift_col][:, None, None]
            )
    centre = filtered - jnp.mean(filtered, axis=0, keepdims=True)
    spread = jnp.mean(centre * centre, axis=0, keepdims=True)
    normed = (
        centre * lax.rsqrt(spread + 1e-06) * norm_gain[:, None, None] + norm_bias[:, None, None]
    ).astype(jnp.bfloat16)
    hidden = (
        jnp.einsum("cpq,ck->kpq", normed, w_up, preferred_element_type=jnp.float32)
        + up_bias[:, None, None]
    )
    hidden = jax.nn.gelu(hidden, approximate=False).astype(jnp.bfloat16)
    update = (
        jnp.einsum("kpq,kc->cpq", hidden, w_down, preferred_element_type=jnp.float32)
        + down_bias[:, None, None]
    )
    return (mixed.astype(jnp.float32) + layer_scale[:, None, None] * update).astype(jnp.bfloat16)


def solution(mesh):
    return jax.shard_map(
        local,
        mesh=mesh,
        in_specs=(
            P(None, "lat", "lon"),
            P(None, ("lat", "lon")),
            P(None, ("lat", "lon")),
            P(("lat", "lon")),
            P(("lat", "lon")),
            P(),
            P(),
            P(),
            P(),
            P(),
            P(),
            P(),
            P(),
            P(),
            P(),
        ),
        out_specs=P(None, "lat", "lon"),
        check_vma=False,
    )
```

profile of v0, /device:TPU:23, one launch (start us, length us, event | category | flops | bytes accessed | tf_op | source)
XLA Modules:
  0.0 150.3 jit_solution(11679636226880003412)
XLA Ops:
  0.7 0.7 fusion.119
  1.5 1.8 %concatenate.79 = f32[69,2048]{1,0:T(8,128)S(1)} concatenate(bf16[64,2048]{1,0:T(8,128)(2,1)} %param.18, f32[2,2048]{1,0:T(2,128)} %param.19, f32[1,2048]{1,0:T(1,128)S(1)} %bitcast.159, f32[1,2048]{1,0:T(1,128)S(1)} %bitcast.158, f32[1,2048]{1,0:T(1,128)S(1)} %compare_convert_fusion), dimensions={0} | concatenate | bytes 868352 | tf_op jit(solution)/shard_map/concatenate | solution.py:76
  3.3 0.1 broadcast_in_dim.45
  3.4 3.7 %while.15 = (s32[]{:T(128)}, f32[2048,136]{0,1:T(8,128)S(1)}, f32[32,136]{1,0:T(8,128)S(1)}, s32[]{:T(128)}, f32[69,2048]{1,0:T(8,128)S(1)}, /*index=5*/s32[]{:T...) while((s32[]{:T(128)}, f32[2048,136]{0,1:T(8,128)S(1)}, ...), condition=%wide.region_1.2_spmd, body=%wide.region_0.1_spmd.sunk | while | flops 79286192 | bytes 3453667 | solution.py:66
  3.4 0.1 fusion.173
  3.5 0.7 add_compare_fusion.2
  4.2 0.1 fusion.174
  4.3 0.1 multiply_convert_fusion.2
  4.4 0.5 convolution_add_fusion.4
  4.9 0.3 convolution_add_fusion.5
  5.3 0.1 fusion.173
  5.4 0.7 add_compare_fusion.2
  6.0 0.1 fusion.174
  6.2 0.1 multiply_convert_fusion.2
  6.3 0.5 convolution_add_fusion.4
  6.8 0.3 convolution_add_fusion.5
  7.1 1.8 %copy.23 = f32[2048,136]{1,0:T(8,128)} copy(f32[2048,136]{0,1:T(8,128)S(1)} %get-tuple-element.111) | data formatting | bytes 2228224 | tf_op jit(solution)/shard_map/while | solution.py:66
  8.9 2.8 %copy_dynamic-update-slice_fusion = f32[65,32,136]{2,0,1:T(8,128)S(1)} fusion(f32[64,32,136]{2,1,0:T(8,128)} %bitcast.157), kind=kLoop, calls=%fused_computation.120 | loop fusion | bytes 3211264
  11.8 0.1 dynamic-update-slice.1
  11.9 0.1 convert_element_type.257
  12.0 0.0 copy-start.2
  12.1 1.0 copy-done.2
  13.1 1.1 fusion.157
  14.2 1.4 copy.25
  15.6 1.7 %collective-permute-start = (bf16[65,32,4]{0,1,2:T(8,128)(2,1)S(1)}, bf16[65,32,4]{0,1,2:T(8,128)(2,1)S(1)}, u32[]{:S(2)}, u32[]{:S(2)}) collective-permute-start(bf16[65,32,4]{0,1,2:T(8,128)(2,1)S(1)} %copy.25), channel_id=1, source_target_pairs={{0,1},{1,2},{2,3},{3,4},{4,5},{5,6},{6,7},{7,8},{8,9},{9,10},{10,1... | collective-permute-start | bytes 49928 | tf_op jit(solution)/shard_map/ppermute | solution.py:21
  17.3 1.0 copy.26
  18.2 4.8 %collective-permute-start.1 = (bf16[65,32,4]{0,1,2:T(8,128)(2,1)}, bf16[65,32,4]{0,1,2:T(8,128)(2,1)}, u32[]{:S(2)}, u32[]{:S(2)}) collective-permute-start(bf16[65,32,4]{0,1,2:T(8,128)(2,1)} %copy.26), channel_id=1, source_target_pairs={{1,0},{2,1},{3,2},{4,3},{5,4},{6,5},{7,6},{8,7},{9,8},{10,9},{11,1... | collective-permute-start | bytes 49928 | tf_op jit(solution)/shard_map/ppermute | solution.py:22
  23.0 1.4 slice.550
  24.4 0.4 copy.27
  24.8 0.0 collective-permute-done.1
  24.8 1.9 %copy.28 = bf16[65,32,4]{2,0,1:T(8,128)(2,1)} copy(bf16[65,32,4]{0,1,2:T(8,128)(2,1)} %collective-permute-done.1) | data formatting | bytes 33280 | tf_op jit(solution)/shard_map/ppermute | solution.py:22
  26.8 2.2 %maximum_convert_fusion = f32[65,32,144]{2,0,1:T(8,128)S(1)} fusion(bf16[65,32,4]{2,0,1:T(8,128)(2,1)} %copy.28, bf16[65,32,136]{2,0,1:T(8,128)(2,1)} %copy-done.2, bf16[65,32,4]{2,0,1:T(8,128)(2,1)S(1)} %copy.27), kind=kLoop, calls=%fused_computation.135 | loop fusion | flops 1797120 | bytes 1797120 | tf_op jit(solution)/shard_map/convert_element_type | solution.py:89
  29.0 0.7 slice_add_fusion.1
  29.7 0.0 copy-start.4
  29.7 0.6 copy-done.3
  30.3 0.7 fusion.155
  30.9 0.0 copy-start.5
  31.0 3.2 %collective-permute-start.2 = (bf16[65,4,128]{2,0,1:T(8,128)(2,1)S(1)}, bf16[65,4,128]{2,0,1:T(8,128)(2,1)S(1)}, u32[]{:S(2)}, u32[]{:S(2)}) collective-permute-start(bf16[65,4,128]{2,0,1:T(8,128)(2,1)S(1)} %get-tuple-element.145), channel_id=1, source_target_pairs={{0,16},{16,32},{32,48},{48,64},{64,80},{80,96},{96,112},{112,128},... | collective-permute-start | bytes 199688 | tf_op jit(solution)/shard_map/ppermute | solution.py:21
  34.2 1.9 %collective-permute-start.3 = (bf16[65,4,128]{2,0,1:T(8,128)(2,1)S(1)}, bf16[65,4,128]{2,0,1:T(8,128)(2,1)S(1)}, u32[]{:S(2)}, u32[]{:S(2)}) collective-permute-start(bf16[65,4,128]{2,0,1:T(8,128)(2,1)S(1)} %get-tuple-element.146), channel_id=1, source_target_pairs={{16,0},{32,16},{48,32},{64,48},{80,64},{96,80},{112,96},{128,112},... | collective-permute-start | bytes 199688 | tf_op jit(solution)/shard_map/ppermute | solution.py:22
  36.2 2.8 %copy.22 = bf16[256,24,128]{0,2,1:T(8,128)(2,1)} copy(bf16[256,24,128]{2,1,0:T(8,128)(2,1)} %param.17) | data formatting | bytes 3145728 | tf_op args[0]
  39.0 1.8 %collective-permute-done.3 = bf16[65,4,128]{2,0,1:T(8,128)(2,1)S(1)} collective-permute-done((bf16[65,4,128]{2,0,1:T(8,128)(2,1)S(1)}, bf16[65,4,128]{2,0,1:T(8,128)(2,1)S(1)}, u32[]{:S(2)}, u32[]{:S(2)}) %collective-permute-start.3) | collective-permute-done | bytes 66592 | tf_op jit(solution)/shard_map/ppermute | solution.py:22
  40.8 2.0 %fusion.92 = bf16[256,24,128]{0,2,1:T(8,128)(2,1)S(1)} fusion(bf16[256,24,128]{0,2,1:T(8,128)(2,1)} %copy.22, bf16[65,4,128]{2,0,1:T(8,128)(2,1)S(1)} %get-tuple-element.136, bf16[65,16,128]{2,0,1:T(8,128)(2,1)S(1)} %slice.556, bf16[65,4,128]{2,0,1:T(8,128)(2,1)S(1)} %get-tuple-element.135, bf16[65,256]{1,0:T(8,128)(2,1)S(1)} %copy-done.5), kind=kOutput, calls=%fused_computation.113 | convolution fusion | flops 104994816 | bytes 3578368 | tf_op jit(solution)/shard_map/spq,sc->cpq/dot_general | solution.py:113
  42.9 0.1 collective-permute-start.4
  43.1 16.9 %collective-permute-start.5 = (bf16[256,24,3]{0,2,1:T(4,128)(2,1)S(1)}, bf16[256,24,3]{0,2,1:T(4,128)(2,1)S(1)}, u32[]{:S(2)}, u32[]{:S(2)}) collective-permute-start(bf16[256,24,3]{0,2,1:T(4,128)(2,1)S(1)} %get-tuple-element.142), channel_id=1, source_target_pairs={{1,0},{2,1},{3,2},{4,3},{5,4},{6,5},{7,6},{8,7},{9,8},{10,9},{11,1... | collective-permute-start | bytes 110600 | tf_op jit(solution)/shard_map/ppermute | solution.py:22
  59.9 1.4 collective-permute-done.4
  61.3 0.0 collective-permute-done.5
  61.3 0.1 pad_maximum_fusion.6
  61.4 0.0 copy-start.6
  61.5 15.9 %collective-permute-start.6 = (bf16[256,3,134]{0,2,1:T(8,128)(2,1)S(1)}, bf16[256,3,134]{0,2,1:T(8,128)(2,1)S(1)}, u32[]{:S(2)}, u32[]{:S(2)}) collective-permute-start(bf16[256,3,134]{0,2,1:T(8,128)(2,1)S(1)} %get-tuple-element.139), channel_id=1, source_target_pairs={{0,16},{16,32},{32,48},{48,64},{64,80},{80,96},{96,112},{112,128},... | collective-permute-start | bytes 617480 | tf_op jit(solution)/shard_map/ppermute | solution.py:21
  77.3 2.1 %collective-permute-start.7 = (bf16[256,3,134]{0,2,1:T(8,128)(2,1)S(1)}, bf16[256,3,134]{0,2,1:T(8,128)(2,1)S(1)}, u32[]{:S(2)}, u32[]{:S(2)}) collective-permute-start(bf16[256,3,134]{0,2,1:T(8,128)(2,1)S(1)} %get-tuple-element.140), channel_id=1, source_target_pairs={{16,0},{32,16},{48,32},{64,48},{80,64},{96,80},{112,96},{128,112},... | collective-permute-start | bytes 617480 | tf_op jit(solution)/shard_map/ppermute | solution.py:22
  79.5 0.6 collective-permute-done.6
  80.1 6.4 %collective-permute-done.7 = bf16[256,3,134]{0,2,1:T(8,128)(2,1)S(1)} collective-permute-done((bf16[256,3,134]{0,2,1:T(8,128)(2,1)S(1)}, bf16[256,3,134]{0,2,1:T(8,128)(2,1)S(1)}, u32[]{:S(2)}, u32[]{:S(2)}) %collective-permute-start.7) | collective-permute-done | bytes 205856 | tf_op jit(solution)/shard_map/ppermute | solution.py:22
  86.4 1.6 %maximum_maximum_fusion = (bf16[256,27,134]{0,2,1:T(8,128)(2,1)S(1)}, bf16[256,27,134]{0,2,1:T(8,128)(2,1)S(1)}) fusion(bf16[256,24,3]{0,2,1:T(4,128)(2,1)S(1)} %collective-permute-done.5, bf16[256,24,128]{0,2,1:T(8,128)(2,1)S(1)} %fusion.92, bf16[256,24,3]{0,2,1:T(4,128)(2,1)S(1)} %collective-permute-done.4, ...), kind=kLoop, calls=%fused_computation.121 | loop fusion | flops 14819328 | bytes 5763072 | tf_op jit(solution)/shard_map/concatenate | solution.py:23
  88.0 24.7 %fusion.153 = (f32[24,128]{1,0:T(8,128)S(1)}, f32[256,24,128]{0,2,1:T(8,128)S(1)}) fusion(f32[256]{0:T(256)S(1)} %bitcast.207, bf16[256,27,134]{0,2,1:T(8,128)(2,1)S(1)} %get-tuple-element.138, f32[256]{0:T(256)S(1)} %bitcast.208, f32[256]{0:T(256)S(1)} %bitcast.161, f32[256]{0:T(256)S(1)} %bitcast.162, f32[256]{0:T(256)S(1)} %bitcast.163, ...), kind=kLoop, calls=%fused_computation.198 | loop fusion | flops 130544640 | bytes 70916096 | tf_op jit(solution)/shard_map/reduce_sum | solution.py:148
  112.8 0.0 copy-start.7
  112.8 0.0 copy-start.8
  112.8 0.0 copy-start.9
  112.8 0.0 copy-start.10
  112.8 0.0 copy-start.11
  112.8 0.0 copy-start.12
  112.9 1.5 %copy-done.1 = f32[256,24,128]{0,2,1:T(8,128)} copy-done((f32[256,24,128]{0,2,1:T(8,128)}, f32[256,24,128]{0,2,1:T(8,128)S(1)}, u32[]{:S(2)}) %copy-start.1) | copy-done | bytes 3145752
  114.4 0.9 multiply_reduce_fusion
  115.4 32.2 %fusion.91 = bf16[256,24,128]{0,2,1:T(8,128)(2,1)} fusion(bf16[256,24,128]{0,2,1:T(8,128)(2,1)S(1)} %fusion.92, f32[1024]{0:T(1024)S(1)} %copy-done.8, f32[256,24,128]{0,2,1:T(8,128)} %copy-done.1, f32[256]{0:T(256)S(1)} %copy-done.9, f32[256]{0:T(256)S(1)} %copy-done.10, f32[256]{0:T(256)S(1)} %copy-done.11, f32[24,128]{1,0:T(8,128)S(1)} %add_rsqrt_fusion, ...), kind=kOutput, calls=%fused_computation.111 | convolution fusion | flops 3436707840 | bytes 7372800 | tf_op jit(solution)/shard_map/kpq,kc->cpq/dot_general | solution.py:159
  147.6 2.7 %copy.29 = bf16[256,24,128]{2,1,0:T(8,128)(2,1)} copy(bf16[256,24,128]{0,2,1:T(8,128)(2,1)} %fusion.91) | data formatting | bytes 3145728 | tf_op jit(solution)/shard_map/convert_element_type | solution.py:162
  (33 shorter events, 0.3 us)
Async XLA Ops:
  0.0 115.3 %copy-start = (bf16[1024,256]{1,0:T(8,128)(2,1)S(1)}, bf16[1024,256]{1,0:T(8,128)(2,1)}, u32[]{:S(2)}) copy-start(bf16[1024,256]{1,0:T(8,128)(2,1)} %param.29) | copy-start | bytes 1572868
  12.0 1.0 copy-start.2
  15.6 8.9 %collective-permute-start = (bf16[65,32,4]{0,1,2:T(8,128)(2,1)S(1)}, bf16[65,32,4]{0,1,2:T(8,128)(2,1)S(1)}, u32[]{:S(2)}, u32[]{:S(2)}) collective-permute-start(bf16[65,32,4]{0,1,2:T(8,128)(2,1)S(1)} %copy.25), channel_id=1, source_target_pairs={{0,1},{1,2},{2,3},{3,4},{4,5},{5,6},{6,7},{7,8},{8,9},{9,10},{10,1... | collective-permute-start | bytes 49928 | tf_op jit(solution)/shard_map/ppermute | solution.py:21
  18.2 6.6 %collective-permute-start.1 = (bf16[65,32,4]{0,1,2:T(8,128)(2,1)}, bf16[65,32,4]{0,1,2:T(8,128)(2,1)}, u32[]{:S(2)}, u32[]{:S(2)}) collective-permute-start(bf16[65,32,4]{0,1,2:T(8,128)(2,1)} %copy.26), channel_id=1, source_target_pairs={{1,0},{2,1},{3,2},{4,3},{5,4},{6,5},{7,6},{8,7},{9,8},{10,9},{11,1... | collective-permute-start | bytes 49928 | tf_op jit(solution)/shard_map/ppermute | solution.py:22
  29.0 1.3 copy-start.3
  29.7 6.5 %copy-start.4 = (f32[256,7,7]{0,2,1:T(8,128)S(1)}, f32[256,7,7]{0,2,1:T(8,128)}, u32[]{:S(2)}) copy-start(f32[256,7,7]{0,2,1:T(8,128)} %param.23) | copy-start | bytes 150532
  30.9 9.9 %copy-start.5 = (bf16[65,256]{1,0:T(8,128)(2,1)S(1)}, bf16[65,256]{1,0:T(8,128)(2,1)}, u32[]{:S(2)}) copy-start(bf16[65,256]{1,0:T(8,128)(2,1)} %param.22) | copy-start | bytes 99844
  31.0 8.1 %collective-permute-start.2 = (bf16[65,4,128]{2,0,1:T(8,128)(2,1)S(1)}, bf16[65,4,128]{2,0,1:T(8,128)(2,1)S(1)}, u32[]{:S(2)}, u32[]{:S(2)}) collective-permute-start(bf16[65,4,128]{2,0,1:T(8,128)(2,1)S(1)} %get-tuple-element.145), channel_id=1, source_target_pairs={{0,16},{16,32},{32,48},{48,64},{64,80},{80,96},{96,112},{112,128},... | collective-permute-start | bytes 199688 | tf_op jit(solution)/shard_map/ppermute | solution.py:21
  34.2 6.6 %collective-permute-start.3 = (bf16[65,4,128]{2,0,1:T(8,128)(2,1)S(1)}, bf16[65,4,128]{2,0,1:T(8,128)(2,1)S(1)}, u32[]{:S(2)}, u32[]{:S(2)}) collective-permute-start(bf16[65,4,128]{2,0,1:T(8,128)(2,1)S(1)} %get-tuple-element.146), channel_id=1, source_target_pairs={{16,0},{32,16},{48,32},{64,48},{80,64},{96,80},{112,96},{128,112},... | collective-permute-start | bytes 199688 | tf_op jit(solution)/shard_map/ppermute | solution.py:22
  42.9 18.4 %collective-permute-start.4 = (bf16[256,24,3]{0,2,1:T(4,128)(2,1)S(1)}, bf16[256,24,3]{0,2,1:T(4,128)(2,1)S(1)}, u32[]{:S(2)}, u32[]{:S(2)}) collective-permute-start(bf16[256,24,3]{0,2,1:T(4,128)(2,1)S(1)} %get-tuple-element.141), channel_id=1, source_target_pairs={{0,1},{1,2},{2,3},{3,4},{4,5},{5,6},{6,7},{7,8},{8,9},{9,10},{10,1... | collective-permute-start | bytes 110600 | tf_op jit(solution)/shard_map/ppermute | solution.py:21
  43.1 18.3 %collective-permute-start.5 = (bf16[256,24,3]{0,2,1:T(4,128)(2,1)S(1)}, bf16[256,24,3]{0,2,1:T(4,128)(2,1)S(1)}, u32[]{:S(2)}, u32[]{:S(2)}) collective-permute-start(bf16[256,24,3]{0,2,1:T(4,128)(2,1)S(1)} %get-tuple-element.142), channel_id=1, source_target_pairs={{1,0},{2,1},{3,2},{4,3},{5,4},{6,5},{7,6},{8,7},{9,8},{10,9},{11,1... | collective-permute-start | bytes 110600 | tf_op jit(solution)/shard_map/ppermute | solution.py:22
  61.4 26.6 %copy-start.6 = (f32[256]{0:T(256)S(1)}, f32[256]{0:T(256)}, u32[]{:S(2)}) copy-start(f32[256]{0:T(256)} %param.24) | copy-start | bytes 3076
  61.5 18.6 %collective-permute-start.6 = (bf16[256,3,134]{0,2,1:T(8,128)(2,1)S(1)}, bf16[256,3,134]{0,2,1:T(8,128)(2,1)S(1)}, u32[]{:S(2)}, u32[]{:S(2)}) collective-permute-start(bf16[256,3,134]{0,2,1:T(8,128)(2,1)S(1)} %get-tuple-element.139), channel_id=1, source_target_pairs={{0,16},{16,32},{32,48},{48,64},{64,80},{80,96},{96,112},{112,128},... | collective-permute-start | bytes 617480 | tf_op jit(solution)/shard_map/ppermute | solution.py:21
  77.3 9.1 %collective-permute-start.7 = (bf16[256,3,134]{0,2,1:T(8,128)(2,1)S(1)}, bf16[256,3,134]{0,2,1:T(8,128)(2,1)S(1)}, u32[]{:S(2)}, u32[]{:S(2)}) collective-permute-start(bf16[256,3,134]{0,2,1:T(8,128)(2,1)S(1)} %get-tuple-element.140), channel_id=1, source_target_pairs={{16,0},{32,16},{48,32},{64,48},{80,64},{96,80},{112,96},{128,112},... | collective-permute-start | bytes 617480 | tf_op jit(solution)/shard_map/ppermute | solution.py:22
  112.8 1.6 %copy-start.1 = (f32[256,24,128]{0,2,1:T(8,128)}, f32[256,24,128]{0,2,1:T(8,128)S(1)}, u32[]{:S(2)}) copy-start(f32[256,24,128]{0,2,1:T(8,128)S(1)} %get-tuple-element.126) | copy-start | bytes 9437188
  112.8 2.6 %copy-start.7 = (bf16[256,1024]{1,0:T(8,128)(2,1)S(1)}, bf16[256,1024]{1,0:T(8,128)(2,1)}, u32[]{:S(2)}) copy-start(bf16[256,1024]{1,0:T(8,128)(2,1)} %param.27) | copy-start | bytes 1572868
  112.8 2.6 %copy-start.8 = (f32[1024]{0:T(1024)S(1)}, f32[1024]{0:T(1024)}, u32[]{:S(2)}) copy-start(f32[1024]{0:T(1024)} %param.28) | copy-start | bytes 12292
  112.8 2.6 %copy-start.9 = (f32[256]{0:T(256)S(1)}, f32[256]{0:T(256)}, u32[]{:S(2)}) copy-start(f32[256]{0:T(256)} %param.30) | copy-start | bytes 3076
  112.8 2.6 %copy-start.10 = (f32[256]{0:T(256)S(1)}, f32[256]{0:T(256)}, u32[]{:S(2)}) copy-start(f32[256]{0:T(256)} %param.26) | copy-start | bytes 3076
  112.8 2.6 %copy-start.11 = (f32[256]{0:T(256)S(1)}, f32[256]{0:T(256)}, u32[]{:S(2)}) copy-start(f32[256]{0:T(256)} %param.25) | copy-start | bytes 3076
  112.8 2.6 %copy-start.12 = (f32[256]{0:T(256)S(1)}, f32[256]{0:T(256)}, u32[]{:S(2)}) copy-start(f32[256]{0:T(256)} %param.31) | copy-start | bytes 3076
where the time goes:
time: 153 us; the launch traced here: 150 us
  starting transfers between devices  46.6 us (30%)
  matrix products  35.9 us (23%)
  other arithmetic  33.7 us (22%)
  local copies, waits for them, and re-layouts  22.7 us (15%)
  waiting for transfers between devices  10.1 us (7%)
    dot_general x1, matrix products, local(): jnp.einsum('kpq,kc->cpq', hidden, w_down, preferred_element_type=jnp.floa...  32.2 us
    ppermute x4, starting transfers between devices, with_halo(): after = lax.ppermute(initial, axis, down)  25.7 us
    reduce_sum x1, other arithmetic, local(): centre = filtered - jnp.mean(filtered, axis=0, keepdims=True)  24.7 us
    ppermute x4, starting transfers between devices, with_halo(): before = lax.ppermute(last, axis, up)  21 us
    unnamed x28, local copies, waits for them, and re-layouts  8.79 us
    ppermute x4, waiting for transfers between devices, with_halo(): after = lax.ppermute(initial, axis, down)  8.13 us
  transfers between devices with their start and end apart: 8, of which 4 were waited for; matrix products, arithmetic and copies ran while one was open for 4% of the time, Pallas kernels for 0%

commit v1 on v0

--- a/solution.py
+++ b/solution.py
@@ -1,6 +1,8 @@
 import jax
 import jax.numpy as jnp
 from jax import lax
+from jax.experimental import pallas as pl
+from jax.experimental.pallas import tpu as pltpu
 from jax.sharding import PartitionSpec as P
 
 KERNEL = 7
@@ -114,6 +116,119 @@
     return (state.astype(jnp.float32) + projected).astype(jnp.bfloat16)
 
 
+BF = jnp.bfloat16
+F = jnp.float32
+CB=16
+RB=4
+
+def shift_matrix():
+    lane = lax.broadcasted_iota(jnp.int32,(256,768),0)
+    out = lax.broadcasted_iota(jnp.int32,(256,768),1)
+    col = jnp.where(lane<128, lane, jnp.where(lane<132, lane-132, lane-4))
+    k = out//128
+    d = jnp.where(k<3, k-3, k-2)
+    return jnp.where((col == out%128 + d) & (lane<136), 1.0, 0.0).astype(BF)
+
+def block_kernel(dwb, gain, nbias, db, ls, mixed, toe, w1, b1, w2, out, xs, filt, xbuf, obuf, smat):
+    f32=jnp.float32
+    smat[...] = shift_matrix()
+    def filt_step(i, s1):
+        c0 = i*CB
+        m = mixed[pl.ds(c0,CB)].reshape(CB*32,256)
+        for j in range(3):
+            z = jnp.dot(m, smat[:, j*256:(j+1)*256], preferred_element_type=f32).astype(BF)
+            for hf in range(2):
+                k = 2*j+hf
+                v = k if k<3 else k+1
+                zz = z[:, hf*128:(hf+1)*128]
+                for c in range(CB):
+                    xs[c//2, v*32:(v+1)*32, (c%2)*128:(c%2)*128+128] = zz[c*32:(c+1)*32]
+        for c in range(CB):
+            xs[c//2, 96:128, (c%2)*128:(c%2)*128+128] = m[c*32:(c+1)*32,:128]
+        for k in range(CB//2):
+            o = jnp.dot(toe[i*(CB//2)+k], xs[k], preferred_element_type=f32)
+            a = o[:24,:128] + dwb[c0+2*k]
+            b = o[24:,128:] + dwb[c0+2*k+1]
+            filt[c0+2*k] = a
+            filt[c0+2*k+1] = b
+            s1 = s1 + (a + b)
+        return s1
+    s1 = lax.fori_loop(0,256//CB,filt_step,jnp.zeros((24,128),f32))
+    mean = s1*(1.0/256)
+    def var_step(i, s2):
+        for k in range(16):
+            a = filt[i*16+k]-mean
+            s2 = s2 + a*a
+        return s2
+    s2 = lax.fori_loop(0,16,var_step,jnp.zeros((24,128),f32))
+    rstd = lax.rsqrt(s2*(1.0/256)+1e-6)
+    def norm_step(i,_):
+        c0=i*16
+        ys=[]
+        for k in range(16):
+            ys.append(((filt[c0+k]-mean)*rstd)*gain[c0+k]+nbias[c0+k])
+        y = jnp.stack(ys,0)
+        xbuf[:, pl.ds(pl.multiple_of(c0,16),16), :] = jnp.swapaxes(y,0,1).astype(BF)
+        return 0
+    lax.fori_loop(0,16,norm_step,0)
+    def mlp_step(i,_):
+        x = jnp.concatenate([xbuf[i*RB+k] for k in range(RB)],1)
+        h = jnp.dot(w1[...], x, preferred_element_type=f32)
+        gs = []
+        for k in range(8):
+            hk = h[k*128:(k+1)*128] + b1[:, k:k+1]
+            gs.append(((0.5*hk)*(1.0+lax.erf(hk*0.7071067811865476))).astype(BF))
+        g = jnp.concatenate(gs, 0)
+        o = jnp.dot(w2[...], g, preferred_element_type=f32)
+        for k in range(RB):
+            obuf[i*RB+k] = o[:,k*128:(k+1)*128]
+        return 0
+    lax.fori_loop(0,24//RB,mlp_step,0)
+    def out_step(i,_):
+        c0=pl.multiple_of(i*16,16)
+        o = jnp.swapaxes(obuf[:, pl.ds(c0,16), :],0,1)
+        m = mixed[pl.ds(c0,16), 4:28, :128].astype(f32)
+        for k in range(16):
+            out[c0+k] = (m[k] + (o[k] + db[c0+k])*ls[c0+k]).astype(BF)
+        return 0
+    lax.fori_loop(0,16,out_step,0)
+
+
+def prepare_kernel(base, w_up, w_down, b1, toe, w1, w2, b1c):
+    w1[...] = w_up[...].T
+    w2[...] = w_down[...].T
+    b1c[...] = b1[...].T
+    def step(i,_):
+        rows = base[pl.ds(pl.multiple_of(i*8,8),8), :]
+        for k in range(8):
+            parts=[]
+            for ln in range(2):
+                b = jnp.broadcast_to(rows[k:k+1, ln*128:(ln+1)*128],(24,128))
+                parts.append(pltpu.roll(b, 0, 1, stride=1, stride_axis=0))
+            y = jnp.concatenate(parts,1).astype(BF)
+            toe[i*4+k//2, (k%2)*24:(k%2)*24+24, :] = y[:, :224]
+        return 0
+    lax.fori_loop(0,32,step,0)
+
+
+def prepare(dw_weight, w_up, w_down, up_bias):
+    base = jnp.pad(jnp.swapaxes(dw_weight,1,2), ((0,0),(0,1),(1,24))).reshape(256,256)
+    S = jax.ShapeDtypeStruct
+    return pl.pallas_call(prepare_kernel, name="prepare",
+        out_shape=(S((128,48,224),BF), S((1024,256),BF), S((256,1024),BF), S((128,8),F)),
+        compiler_params=pltpu.CompilerParams(vmem_limit_bytes=40*2**20))(base, w_up, w_down, up_bias.reshape(8,128))
+
+
+def block(mixed, toe, w1, w2, b1, dw_bias, norm_gain, norm_bias, down_bias, layer_scale):
+    S=pl.BlockSpec(memory_space=pltpu.SMEM)
+    V=pl.BlockSpec(memory_space=pltpu.VMEM)
+    return pl.pallas_call(block_kernel, out_shape=jax.ShapeDtypeStruct((256,24,128),BF), name="block",
+        in_specs=[S]*5+[V]*5, out_specs=V,
+        scratch_shapes=[pltpu.VMEM((CB//2,224,256),BF), pltpu.VMEM((256,24,128),F), pltpu.VMEM((24,256,128),BF), pltpu.VMEM((24,256,128),F), pltpu.VMEM((256,768),BF)],
+        compiler_params=pltpu.CompilerParams(vmem_limit_bytes=58*2**20))(
+        dw_bias, norm_gain, norm_bias, down_bias, layer_scale, mixed, toe, w1, b1, w2)
+
+
 def local(
     state,
     obs_values,
@@ -137,29 +252,11 @@
     mixed = encode(sources, state, w_in)
     mixed_wide = with_halo(mixed, (("lon", 2),), margin, True)
     padded = with_halo(mixed_wide, (("lat", 1),), margin, False)
-    filtered = jnp.zeros((channels, rows_tile, cols_tile), jnp.float32) + dw_bias[:, None, None]
-    for shift_row in range(KERNEL):
-        for shift_col in range(KERNEL):
-            window = padded[:, shift_row : shift_row + rows_tile, shift_col : shift_col + cols_tile]
-            filtered = (
-                filtered
-                + window.astype(jnp.float32) * dw_weight[:, shift_row, shift_col][:, None, None]
-            )
-    centre = filtered - jnp.mean(filtered, axis=0, keepdims=True)
-    spread = jnp.mean(centre * centre, axis=0, keepdims=True)
-    normed = (
-        centre * lax.rsqrt(spread + 1e-06) * norm_gain[:, None, None] + norm_bias[:, None, None]
-    ).astype(jnp.bfloat16)
-    hidden = (
-        jnp.einsum("cpq,ck->kpq", normed, w_up, preferred_element_type=jnp.float32)
-        + up_bias[:, None, None]
-    )
-    hidden = jax.nn.gelu(hidden, approximate=False).astype(jnp.bfloat16)
-    update = (
-        jnp.einsum("kpq,kc->cpq", hidden, w_down, preferred_element_type=jnp.float32)
-        + down_bias[:, None, None]
-    )
-    return (mixed.astype(jnp.float32) + layer_scale[:, None, None] * update).astype(jnp.bfloat16)
+    z = lambda n, m: jnp.zeros((channels, n, m), BF)
+    body = jnp.concatenate([padded[:, :, margin:-margin], z(rows_tile+6, 1), padded[:, :, :margin], padded[:, :, -margin:], z(rows_tile+6, 121)], 2)
+    body = jnp.pad(body, ((0,0),(1,1),(0,0)))
+    toe, w1, w2, b1 = prepare(dw_weight, w_up, w_down, up_bias)
+    return block(body, toe, w1, w2, b1, dw_bias, norm_gain, norm_bias, down_bias, layer_scale)
 
 
 def solution(mesh):

time: 153 us -> 153 us (level)
  the two profiles are of different devices: /device:TPU:23 before, /device:TPU:16 now
where the time goes in v1:
time: 153 us
  local copies, waits for them, and re-layouts  55 us (36%)
  starting transfers between devices  34.9 us (23%)
  Pallas kernels  27.5 us (18%)
  other arithmetic  21 us (14%)
  matrix products  10.8 us (7%)
  waiting for transfers between devices  2.02 us (1%)
    ppermute x4, starting transfers between devices, with_halo(): after = lax.ppermute(initial, axis, down)  25.2 us
    pallas_call x1, Pallas kernels, block(): pl.pallas_call(block_kernel, out_shape=jax.ShapeDtypeStruct((256, 24, 128...  24.1 us
    unnamed x28, local copies, waits for them, and re-layouts  13.9 us
    concatenate x1, local copies, waits for them, and re-layouts, local(): jnp.concatenate([padded[:, :, margin:-margin], z(rows_tile + 6, 1), padde...  12.2 us
    ppermute x4, starting transfers between devices, with_halo(): before = lax.ppermute(last, axis, up)  9.65 us
    lt x12, other arithmetic, add_block(): live_rows = row_start + lax.iota(jnp.int32, BLOCK) < live_count  7.81 us
    pad x1, local copies, waits for them, and re-layouts, local(): body = jnp.pad(body, ((0, 0), (1, 1), (0, 0)))  6.59 us
    dot_general x12, matrix products, add_block(): lax.dot_general(scaled, lon_weight.astype(jnp.bfloat16), contract, prefer...  6.06 us
  transfers between devices with their start and end apart: 8, of which 2 were waited for; matrix products, arithmetic and copies ran while one was open for 3% of the time, Pallas kernels for 2%

profile of v1, /device:TPU:16, one launch (start us, length us, event | category | flops | bytes accessed | tf_op | source)
XLA Modules:
  0.0 153.2 jit_solution(13488107508932605239)
XLA Ops:
  0.7 0.7 fusion.54
  1.4 1.8 %concatenate.28 = f32[69,2048]{1,0:T(8,128)S(1)} concatenate(bf16[64,2048]{1,0:T(8,128)(2,1)} %param.18, f32[2,2048]{1,0:T(2,128)} %param.19, f32[1,2048]{1,0:T(1,128)S(1)} %bitcast.40, f32[1,2048]{1,0:T(1,128)S(1)} %bitcast.39, f32[1,2048]{1,0:T(1,128)S(1)} %compare_convert_fusion), dimensions={0} | concatenate | bytes 868352 | tf_op jit(solution)/shard_map/concatenate | solution.py:78
  3.3 22.4 %while.15 = (s32[]{:T(128)}, f32[2048,136]{0,1:T(8,128)S(1)}, f32[32,136]{1,0:T(8,128)S(1)}, s32[]{:T(128)}, f32[69,2048]{1,0:T(8,128)S(1)}, /*index=5*/s32[]{:T...) while((s32[]{:T(128)}, f32[2048,136]{0,1:T(8,128)S(1)}, ...), condition=%wide.region_1.2_spmd, body=%wide.region_0.1_spmd.sunk | while | flops 79286192 | bytes 3453667 | solution.py:68
  3.5 0.7 add_compare_fusion.2
  4.3 0.5 convolution_add_fusion.4
  5.3 0.7 add_compare_fusion.2
  6.2 0.5 convolution_add_fusion.4
  7.2 0.7 add_compare_fusion.2
  9.1 0.7 add_compare_fusion.2
  9.9 0.5 convolution_add_fusion.4
  10.9 0.7 add_compare_fusion.2
  11.8 0.5 convolution_add_fusion.4
  12.8 0.7 add_compare_fusion.2
  14.7 0.7 add_compare_fusion.2
  15.6 0.5 convolution_add_fusion.4
  16.5 0.7 add_compare_fusion.2
  17.4 0.5 convolution_add_fusion.4
  18.4 0.7 add_compare_fusion.2
  19.3 0.5 convolution_add_fusion.4
  20.3 0.7 add_compare_fusion.2
  21.2 0.5 convolution_add_fusion.4
  22.1 0.7 add_compare_fusion.2
  23.0 0.5 convolution_add_fusion.4
  24.0 0.7 add_compare_fusion.2
  24.9 0.5 convolution_add_fusion.4
  25.8 1.8 %copy.24 = f32[2048,136]{1,0:T(8,128)} copy(f32[2048,136]{0,1:T(8,128)S(1)} %get-tuple-element.115) | data formatting | bytes 2228224 | tf_op jit(solution)/shard_map/while | solution.py:68
  27.6 2.8 %copy_dynamic-update-slice_fusion = f32[65,32,136]{2,0,1:T(8,128)S(1)} fusion(f32[64,32,136]{2,1,0:T(8,128)} %bitcast.36), kind=kLoop, calls=%fused_computation.60 | loop fusion | bytes 3211264
  30.7 1.0 copy-done.8
  31.7 1.1 fusion.60
  32.8 1.4 copy.26
  34.2 5.7 %collective-permute-start = (bf16[65,32,4]{0,1,2:T(8,128)(2,1)S(1)}, bf16[65,32,4]{0,1,2:T(8,128)(2,1)S(1)}, u32[]{:S(2)}, u32[]{:S(2)}) collective-permute-start(bf16[65,32,4]{0,1,2:T(8,128)(2,1)S(1)} %copy.26), channel_id=1, source_target_pairs={{0,1},{1,2},{2,3},{3,4},{4,5},{5,6},{6,7},{7,8},{8,9},{9,10},{10,1... | collective-permute-start | bytes 49928 | tf_op jit(solution)/shard_map/ppermute | solution.py:23
  40.3 10.2 %collective-permute-start.1 = (bf16[65,32,4]{0,1,2:T(8,128)(2,1)S(1)}, bf16[65,32,4]{0,1,2:T(8,128)(2,1)S(1)}, u32[]{:S(2)}, u32[]{:S(2)}) collective-permute-start(bf16[65,32,4]{0,1,2:T(8,128)(2,1)S(1)} %copy.27), channel_id=1, source_target_pairs={{1,0},{2,1},{3,2},{4,3},{5,4},{6,5},{7,6},{8,7},{9,8},{10,9},{11,1... | collective-permute-start | bytes 49928 | tf_op jit(solution)/shard_map/ppermute | solution.py:24
  50.5 1.4 slice.126
  52.3 1.2 copy.29
  53.5 2.2 %maximum_convert_fusion = f32[65,32,144]{2,0,1:T(8,128)S(1)} fusion(bf16[65,32,4]{2,0,1:T(8,128)(2,1)} %copy.29, bf16[65,32,136]{2,0,1:T(8,128)(2,1)} %copy-done.8, bf16[65,32,4]{2,0,1:T(8,128)(2,1)S(1)} %copy.28), kind=kLoop, calls=%fused_computation.64 | loop fusion | flops 1797120 | bytes 1797120 | tf_op jit(solution)/shard_map/convert_element_type | solution.py:91
  55.8 0.7 slice_add_fusion.1
  56.4 0.6 copy-done.10
  57.0 1.7 %fusion.58 = (bf16[65,32,128]{2,0,1:T(8,128)(2,1)S(1)}, f32[65,32,128]{2,0,1:T(8,128)}) fusion(f32[65,32,4]{2,0,1:T(8,128)S(1)} %get-tuple-element.140, f32[65,32,120]{2,0,1:T(8,128)S(1)} %copy-done.10, f32[65,32,4]{2,0,1:T(8,128)S(1)} %get-tuple-element.139), kind=kLoop, calls=%fused_computation.96 | loop fusion | flops 798720 | bytes 2662400 | tf_op jit(solution)/shard_map/convert_element_type | solution.py:102
  58.7 1.9 %collective-permute-start.2 = (bf16[65,4,128]{2,0,1:T(8,128)(2,1)S(1)}, bf16[65,4,128]{2,0,1:T(8,128)(2,1)S(1)}, u32[]{:S(2)}, u32[]{:S(2)}) collective-permute-start(bf16[65,4,128]{2,0,1:T(8,128)(2,1)S(1)} %get-tuple-element.151), channel_id=1, source_target_pairs={{0,16},{16,32},{32,48},{48,64},{64,80},{80,96},{96,112},{112,128},... | collective-permute-start | bytes 199688 | tf_op jit(solution)/shard_map/ppermute | solution.py:23
  60.7 4.5 %collective-permute-start.3 = (bf16[65,4,128]{2,0,1:T(8,128)(2,1)S(1)}, bf16[65,4,128]{2,0,1:T(8,128)(2,1)S(1)}, u32[]{:S(2)}, u32[]{:S(2)}) collective-permute-start(bf16[65,4,128]{2,0,1:T(8,128)(2,1)S(1)} %get-tuple-element.152), channel_id=1, source_target_pairs={{16,0},{32,16},{48,32},{64,48},{80,64},{96,80},{112,96},{128,112},... | collective-permute-start | bytes 199688 | tf_op jit(solution)/shard_map/ppermute | solution.py:24
  65.2 2.1 %copy.23 = bf16[256,24,128]{0,2,1:T(8,128)(2,1)S(1)} copy(bf16[256,24,128]{2,1,0:T(8,128)(2,1)} %param.17) | data formatting | bytes 3145728 | tf_op args[0]
  67.4 1.0 fusion.51
  68.5 0.6 fusion.44
  69.3 5.8 %collective-permute-start.5 = (bf16[256,24,3]{0,1,2:T(8,128)(2,1)S(1)}, bf16[256,24,3]{0,1,2:T(8,128)(2,1)S(1)}, u32[]{:S(2)}, u32[]{:S(2)}) collective-permute-start(bf16[256,24,3]{0,1,2:T(8,128)(2,1)S(1)} %copy.31), channel_id=1, source_target_pairs={{1,0},{2,1},{3,2},{4,3},{5,4},{6,5},{7,6},{8,7},{9,8},{10,9},{11,1... | collective-permute-start | bytes 110600 | tf_op jit(solution)/shard_map/ppermute | solution.py:24
  75.1 1.9 %collective-permute-done.4 = bf16[256,24,3]{0,1,2:T(8,128)(2,1)S(1)} collective-permute-done((bf16[256,24,3]{0,1,2:T(8,128)(2,1)S(1)}, bf16[256,24,3]{0,1,2:T(8,128)(2,1)S(1)}, u32[]{:S(2)}, u32[]{:S(2)}) %collective-permute-start.4) | collective-permute-done | bytes 36896 | tf_op jit(solution)/shard_map/ppermute | solution.py:23
  77.1 0.9 pad_maximum_fusion.4
  77.9 1.9 %collective-permute-start.6 = (bf16[256,3,134]{0,2,1:T(8,128)(2,1)}, bf16[256,3,134]{0,2,1:T(8,128)(2,1)S(1)}, u32[]{:S(2)}, u32[]{:S(2)}) collective-permute-start(bf16[256,3,134]{0,2,1:T(8,128)(2,1)} %get-tuple-element.145), channel_id=1, source_target_pairs={{0,16},{16,32},{32,48},{48,64},{64,80},{80,96},{96,112},{112,128},... | collective-permute-start | bytes 617480 | tf_op jit(solution)/shard_map/ppermute | solution.py:23
  79.9 4.7 %collective-permute-start.7 = (bf16[256,3,134]{0,2,1:T(8,128)(2,1)}, bf16[256,3,134]{0,2,1:T(8,128)(2,1)}, u32[]{:S(2)}, u32[]{:S(2)}) collective-permute-start(bf16[256,3,134]{0,2,1:T(8,128)(2,1)} %get-tuple-element.146), channel_id=1, source_target_pairs={{16,0},{32,16},{48,32},{64,48},{80,64},{96,80},{112,96},{128,112},... | collective-permute-start | bytes 617480 | tf_op jit(solution)/shard_map/ppermute | solution.py:24
  84.8 3.4 %prepare.1 = (bf16[128,48,224]{2,1,0:T(8,128)(2,1)S(1)}, bf16[1024,256]{1,0:T(8,128)(2,1)S(1)}, bf16[256,1024]{1,0:T(8,128)(2,1)S(1)}, f32[128,8]{1,0:T(8,128)S(1)}) custom-call(f32[256,256]{1,0:T(8,128)S(1)} %copy.38.base, bf16[256,1024]{1,0:T(8,128)(2,1)S(1)} %copy-done.4, bf16[1024,256]{1,0:T(8,128)(2,1)S(1)} %copy-done.5, f32[8,128]{1,0:T(8,128)S(1)} %bitcast.34), custom_call_target="tpu_custom_call" | custom-call | tf_op jit(solution)/shard_map/prepare/pallas_call | solution.py:217
  88.3 1.7 %copy-done.1 = bf16[128,48,224]{2,1,0:T(8,128)(2,1)} copy-done((bf16[128,48,224]{2,1,0:T(8,128)(2,1)}, bf16[128,48,224]{2,1,0:T(8,128)(2,1)S(1)}, u32[]{:S(2)}) %copy-start.1) | copy-done | bytes 2752536
  89.9 0.8 copy-done.2
  90.7 0.8 copy-done.3
  91.5 0.6 copy-done.6
  92.1 0.8 pad_maximum_fusion.7
  92.9 3.9 %copy.35 = bf16[256,30,3]{2,1,0:T(8,128)(2,1)} copy(bf16[256,30,3]{0,2,1:T(4,128)(2,1)S(1)} %get-tuple-element.142) | data formatting | bytes 92160 | tf_op jit(solution)/shard_map/slice | solution.py:256
  96.9 3.9 %copy.36 = bf16[256,30,3]{2,1,0:T(8,128)(2,1)} copy(bf16[256,30,3]{0,2,1:T(4,128)(2,1)S(1)} %get-tuple-element.141) | data formatting | bytes 92160 | tf_op jit(solution)/shard_map/slice | solution.py:256
  100.8 1.7 %pad_maximum_fusion = bf16[256,30,134]{0,2,1:T(8,128)(2,1)S(1)} fusion(bf16[256,3,134]{0,2,1:T(8,128)(2,1)} %collective-permute-done.7, bf16[256,24,3]{0,2,1:T(4,128)(2,1)S(1)} %copy.33, bf16[256,24,128]{0,2,1:T(8,128)(2,1)S(1)} %fusion.44, bf16[256,24,3]{0,2,1:T(4,128)(2,1)S(1)} %copy.32, bf16[256,3,134]{0,2,1:T(8,128)(2,1)S(1)} %collective-permute-done.6), kind=kLoop, calls=%fused_computation.61 | loop fusion | flops 10291200 | bytes 4116480 | tf_op jit(solution)/shard_map/concatenate | solution.py:25
  102.5 1.0 slice.136
  103.6 3.5 %copy.39 = bf16[256,30,128]{2,1,0:T(8,128)(2,1)} copy(bf16[256,30,128]{0,2,1:T(8,128)(2,1)S(1)} %slice.136) | data formatting | bytes 3932160
  107.1 1.7 %broadcast_in_dim.48 = bf16[256,30,1]{2,1,0:T(8,128)(2,1)} broadcast(bf16[]{:T(256)} %constant.104.clone.1), dimensions={} | broadcast | bytes 15362 | tf_op jit(solution)/shard_map/broadcast_in_dim | solution.py:255
  108.7 1.6 %broadcast_in_dim.49 = bf16[256,30,121]{2,1,0:T(8,128)(2,1)} broadcast(bf16[]{:T(256)} %constant.104.clone.1), dimensions={} | broadcast | bytes 1858562 | tf_op jit(solution)/shard_map/broadcast_in_dim | solution.py:255
  110.3 12.2 %concatenate.36 = bf16[256,30,256]{2,1,0:T(8,128)(2,1)} concatenate(bf16[256,30,128]{2,1,0:T(8,128)(2,1)} %copy.39, bf16[256,30,1]{2,1,0:T(8,128)(2,1)} %broadcast_in_dim.48, bf16[256,30,3]{2,1,0:T(8,128)(2,1)S(1)} %copy-done.9, bf16[256,30,3]{2,1,0:T(8,128)(2,1)} %copy.36, bf16[256,30,121]{2,1,0:T(8,128)(2,1)} %broadcast_in_dim.49), dimensions={2} | concatenate | bytes 7864320 | tf_op jit(solution)/shard_map/concatenate | solution.py:256
  122.5 6.6 %pad.8.mixed = bf16[256,32,256]{2,1,0:T(8,128)(2,1)} pad(bf16[256,30,256]{2,1,0:T(8,128)(2,1)} %concatenate.36, bf16[]{:T(256)} %constant.104.clone.1), padding=0_0x1_1x0_0 | pad | bytes 8126466 | tf_op jit(solution)/shard_map/jit(_pad)/pad | solution.py:257
  129.1 24.1 %block.1 = bf16[256,24,128]{2,1,0:T(8,128)(2,1)} custom-call(f32[256]{0:T(256)} %dwb.1, f32[256]{0:T(256)} %gain.1, f32[256]{0:T(256)} %nbias.1, f32[256]{0:T(256)} %db.1, f32[256]{0:T(256)} %ls.1, bf16[256,32,256]{2,1,0:T(8,128)(2,1)} %pad.8.mixed, bf16[128,48,224]{2,1,0:T(8,128)(2,1)} %copy-done.1, bf16[1024,256]{1,0:T(8,128)(2,1)} %copy-done.2, ...), custom_call_target="tpu_custom_call" | custom-call | tf_op jit(solution)/shard_map/block/pallas_call | solution.py:225
  (130 shorter events, 10.3 us)
Async XLA Ops:
  0.0 68.4 %copy-start = (bf16[65,256]{1,0:T(8,128)(2,1)S(1)}, bf16[65,256]{1,0:T(8,128)(2,1)}, u32[]{:S(2)}) copy-start(bf16[65,256]{1,0:T(8,128)(2,1)} %param.22) | copy-start | bytes 99844
  30.7 1.0 copy-start.8
  34.2 17.8 %collective-permute-start = (bf16[65,32,4]{0,1,2:T(8,128)(2,1)S(1)}, bf16[65,32,4]{0,1,2:T(8,128)(2,1)S(1)}, u32[]{:S(2)}, u32[]{:S(2)}) collective-permute-start(bf16[65,32,4]{0,1,2:T(8,128)(2,1)S(1)} %copy.26), channel_id=1, source_target_pairs={{0,1},{1,2},{2,3},{3,4},{4,5},{5,6},{6,7},{7,8},{8,9},{9,10},{10,1... | collective-permute-start | bytes 49928 | tf_op jit(solution)/shard_map/ppermute | solution.py:23
  40.3 12.1 %collective-permute-start.1 = (bf16[65,32,4]{0,1,2:T(8,128)(2,1)S(1)}, bf16[65,32,4]{0,1,2:T(8,128)(2,1)S(1)}, u32[]{:S(2)}, u32[]{:S(2)}) collective-permute-start(bf16[65,32,4]{0,1,2:T(8,128)(2,1)S(1)} %copy.27), channel_id=1, source_target_pairs={{1,0},{2,1},{3,2},{4,3},{5,4},{6,5},{7,6},{8,7},{9,8},{10,9},{11,1... | collective-permute-start | bytes 49928 | tf_op jit(solution)/shard_map/ppermute | solution.py:24
  55.8 1.3 copy-start.10
  58.7 8.7 %collective-permute-start.2 = (bf16[65,4,128]{2,0,1:T(8,128)(2,1)S(1)}, bf16[65,4,128]{2,0,1:T(8,128)(2,1)S(1)}, u32[]{:S(2)}, u32[]{:S(2)}) collective-permute-start(bf16[65,4,128]{2,0,1:T(8,128)(2,1)S(1)} %get-tuple-element.151), channel_id=1, source_target_pairs={{0,16},{16,32},{32,48},{48,64},{64,80},{80,96},{96,112},{112,128},... | collective-permute-start | bytes 199688 | tf_op jit(solution)/shard_map/ppermute | solution.py:23
  60.7 6.8 %collective-permute-start.3 = (bf16[65,4,128]{2,0,1:T(8,128)(2,1)S(1)}, bf16[65,4,128]{2,0,1:T(8,128)(2,1)S(1)}, u32[]{:S(2)}, u32[]{:S(2)}) collective-permute-start(bf16[65,4,128]{2,0,1:T(8,128)(2,1)S(1)} %get-tuple-element.152), channel_id=1, source_target_pairs={{16,0},{32,16},{48,32},{64,48},{80,64},{96,80},{112,96},{128,112},... | collective-permute-start | bytes 199688 | tf_op jit(solution)/shard_map/ppermute | solution.py:24
  69.1 15.5 %copy-start.11 = (f32[256,7,7]{0,2,1:T(8,128)S(1)}, f32[256,7,7]{0,2,1:T(8,128)}, u32[]{:S(2)}) copy-start(f32[256,7,7]{0,2,1:T(8,128)} %param.23) | copy-start | bytes 150532
  69.1 15.7 %copy-start.4 = (bf16[256,1024]{1,0:T(8,128)(2,1)S(1)}, bf16[256,1024]{1,0:T(8,128)(2,1)}, u32[]{:S(2)}) copy-start(bf16[256,1024]{1,0:T(8,128)(2,1)} %w_up.1) | copy-start | bytes 1572868
  69.1 15.7 %copy-start.5 = (bf16[1024,256]{1,0:T(8,128)(2,1)S(1)}, bf16[1024,256]{1,0:T(8,128)(2,1)}, u32[]{:S(2)}) copy-start(bf16[1024,256]{1,0:T(8,128)(2,1)} %w_down.1) | copy-start | bytes 1572868
  69.1 15.7 %copy-start.7 = (f32[1024]{0:T(1024)S(1)}, f32[1024]{0:T(1024)}, u32[]{:S(2)}) copy-start(f32[1024]{0:T(1024)} %param.28) | copy-start | bytes 12292
  69.2 7.8 %collective-permute-start.4 = (bf16[256,24,3]{0,1,2:T(8,128)(2,1)S(1)}, bf16[256,24,3]{0,1,2:T(8,128)(2,1)S(1)}, u32[]{:S(2)}, u32[]{:S(2)}) collective-permute-start(bf16[256,24,3]{0,1,2:T(8,128)(2,1)S(1)} %copy.30), channel_id=1, source_target_pairs={{0,1},{1,2},{2,3},{3,4},{4,5},{5,6},{6,7},{7,8},{8,9},{9,10},{10,1... | collective-permute-start | bytes 110600 | tf_op jit(solution)/shard_map/ppermute | solution.py:23
  69.3 7.7 %collective-permute-start.5 = (bf16[256,24,3]{0,1,2:T(8,128)(2,1)S(1)}, bf16[256,24,3]{0,1,2:T(8,128)(2,1)S(1)}, u32[]{:S(2)}, u32[]{:S(2)}) collective-permute-start(bf16[256,24,3]{0,1,2:T(8,128)(2,1)S(1)} %copy.31), channel_id=1, source_target_pairs={{1,0},{2,1},{3,2},{4,3},{5,4},{6,5},{7,6},{8,7},{9,8},{10,9},{11,1... | collective-permute-start | bytes 110600 | tf_op jit(solution)/shard_map/ppermute | solution.py:24
  77.9 14.2 %collective-permute-start.6 = (bf16[256,3,134]{0,2,1:T(8,128)(2,1)}, bf16[256,3,134]{0,2,1:T(8,128)(2,1)S(1)}, u32[]{:S(2)}, u32[]{:S(2)}) collective-permute-start(bf16[256,3,134]{0,2,1:T(8,128)(2,1)} %get-tuple-element.145), channel_id=1, source_target_pairs={{0,16},{16,32},{32,48},{48,64},{64,80},{80,96},{96,112},{112,128},... | collective-permute-start | bytes 617480 | tf_op jit(solution)/shard_map/ppermute | solution.py:23
  79.9 12.3 %collective-permute-start.7 = (bf16[256,3,134]{0,2,1:T(8,128)(2,1)}, bf16[256,3,134]{0,2,1:T(8,128)(2,1)}, u32[]{:S(2)}, u32[]{:S(2)}) collective-permute-start(bf16[256,3,134]{0,2,1:T(8,128)(2,1)} %get-tuple-element.146), channel_id=1, source_target_pairs={{16,0},{32,16},{48,32},{64,48},{80,64},{96,80},{112,96},{128,112},... | collective-permute-start | bytes 617480 | tf_op jit(solution)/shard_map/ppermute | solution.py:24
  88.3 1.7 %copy-start.1 = (bf16[128,48,224]{2,1,0:T(8,128)(2,1)}, bf16[128,48,224]{2,1,0:T(8,128)(2,1)S(1)}, u32[]{:S(2)}) copy-start(bf16[128,48,224]{2,1,0:T(8,128)(2,1)S(1)} %get-tuple-element.117.toe) | copy-start | bytes 8257540
  89.9 0.8 copy-start.2
  90.7 0.8 copy-start.3
  91.5 0.6 copy-start.6
  107.1 3.3 %copy-start.9 = (bf16[256,30,3]{2,1,0:T(8,128)(2,1)S(1)}, bf16[256,30,3]{2,1,0:T(8,128)(2,1)}, u32[]{:S(2)}) copy-start(bf16[256,30,3]{2,1,0:T(8,128)(2,1)} %copy.35) | copy-start | bytes 138244

commit v2 on v0

v2 whole, which is shorter than its diff:
```python
import jax
import jax.numpy as jnp
from jax import lax
from jax.experimental import pallas as pl
from jax.experimental.pallas import tpu as pltpu
from jax.sharding import PartitionSpec as P

W = 4
SRC = 80
ROWS = 32
OBS_BLOCK = 512
GRID_ROWS = 384
CB = 16
RB = 4
BF = jnp.bfloat16
F = jnp.float32
MIB = 2**20
LAT_STATE = 9 * SRC
LAT_MSG = 9 * SRC + 3 * 256
LON_STATE = 2 * SRC
LON_MSG = 2 * SRC + 2 * 256

inverse_width = 1.0 / (2.0 * 1.5 * 1.5)


def lanes(rows):
    return lax.broadcasted_iota(jnp.int32, (rows, 128), 1)


def sums_kernel(count, row_base, vals, offs, cell, state, sums, up, down, scaled, acc):
    live_count = count[0]
    acc[...] = jnp.zeros(acc.shape, F)

    def add_block(b, _):
        k0 = pl.multiple_of(b * OBS_BLOCK, OBS_BLOCK)
        ks = pl.ds(k0, OBS_BLOCK)
        where_cell = cell[:, ks]
        row = where_cell >> 7
        col = where_cell & 127
        slot = lax.broadcasted_iota(jnp.int32, (1, OBS_BLOCK), 1) + k0
        row = jnp.where(slot < live_count, row, -100)

        def weight(offset, place, centre, valid):
            apart = place - centre
            spread = offset - apart.astype(F) - 0.5
            inside = (jnp.abs(apart) <= W) & valid
            return jnp.where(inside, jnp.exp(-spread * spread * inverse_width), 0.0)

        place = lax.broadcasted_iota(jnp.int32, (ROWS, OBS_BLOCK), 0) - W
        on_grid = (place + row_base[0] >= 0) & (place + row_base[0] < GRID_ROWS)
        lat_weight = weight(offs[0:1, ks], place, row, on_grid)
        place = lax.broadcasted_iota(jnp.int32, (136, OBS_BLOCK), 0)
        first = weight(offs[1:2, ks], place, col, place < 128 + W)
        place = lax.broadcasted_iota(jnp.int32, (8, OBS_BLOCK), 0) - 8
        last = weight(offs[1:2, ks], place, col, place >= -W)
        lon_weight = jnp.concatenate([first, jnp.zeros((112, OBS_BLOCK), F), last], 0).astype(BF)
        ones = jnp.where(lax.broadcasted_iota(jnp.int32, (SRC - 64, OBS_BLOCK), 0) == 0, 1.0, 0.0)
        v = jnp.concatenate([vals[:, ks].astype(F), ones], 0)
        for p in range(ROWS):
            scaled[p * SRC:(p + 1) * SRC] = (v * lat_weight[p:p + 1]).astype(BF)
        for m in range(0, ROWS * SRC, 640):
            acc[m:m + 640] += lax.dot_general(
                scaled[m:m + 640], lon_weight, (((1,), (1,)), ((), ())), preferred_element_type=F)
        return 0

    lax.fori_loop(0, (live_count + OBS_BLOCK - 1) // OBS_BLOCK, add_block, 0)
    for p in range(ROWS):
        sums[p] = acc[p * SRC:(p + 1) * SRC].astype(BF)
    for msg, first, state_tile, state_row in ((up, 0, 0, 0), (down, 24, 16, 5)):
        side = jnp.zeros((SRC, 128), F)
        for i in range(8):
            part = acc[(first + i) * SRC:(first + i + 1) * SRC]
            msg[i * SRC:(i + 1) * SRC] = part[:, :128].astype(BF)
            moved = pltpu.roll(part[:, 128:], i * 8 + 4, 1)
            side = jnp.where((lanes(SRC) >> 3) == i, moved, side)
        msg[8 * SRC:9 * SRC] = side.astype(BF)
        for c in range(0, 256, 16):
            x = jnp.swapaxes(state[c:c + 16, state_tile:state_tile + 8, :].astype(F), 0, 1).astype(BF)
            for j in range(3):
                msg[LAT_STATE + j * 256 + c:LAT_STATE + j * 256 + c + 16] = x[state_row + j]


def observation_sums(obs_values, obs_offsets, obs_cell, obs_count, row_base, state):
    S = pl.BlockSpec(memory_space=pltpu.SMEM)
    V = pl.BlockSpec(memory_space=pltpu.VMEM)
    shape = jax.ShapeDtypeStruct
    return pl.pallas_call(
        sums_kernel, name="observation_sums",
        out_shape=(shape((ROWS, SRC, 256), BF), shape((LAT_MSG, 128), BF), shape((LAT_MSG, 128), BF)),
        in_specs=[S, S] + [V] * 4, out_specs=(V,) * 3,
        scratch_shapes=[pltpu.VMEM((ROWS * SRC, OBS_BLOCK), BF), pltpu.VMEM((ROWS * SRC, 256), F)],
        compiler_params=pltpu.CompilerParams(vmem_limit_bytes=32 * MIB),
    )(obs_count, row_base, obs_values, obs_offsets, obs_cell.reshape(1, -1), state)


def rows_kernel(state, rows, rims):
    def turn(i, _):
        c0 = pl.multiple_of(i * 16, 16)
        rows[:, pl.ds(c0, 16), :] = jnp.swapaxes(state[pl.ds(c0, 16)].astype(F), 0, 1).astype(BF)
        return 0

    lax.fori_loop(0, 16, turn, 0)
    for c in range(0, 256, 64):
        packed = [jnp.zeros((64, 128), F) for _ in range(2)]
        for r in range(24):
            p = r + W
            moved = pltpu.roll(rows[r, c:c + 64, :].astype(F), (p % 16) * 8 + 4, 1)
            packed[p // 16] = jnp.where((lanes(64) >> 3) == p % 16, moved, packed[p // 16])
        for k in range(2):
            rims[k * 256 + c:k * 256 + c + 64] = packed[k].astype(BF)


def state_rows(state):
    shape = jax.ShapeDtypeStruct
    return pl.pallas_call(
        rows_kernel, name="state_rows", out_shape=(shape((24, 256, 128), BF), shape((512, 128), BF)),
        cost_estimate=pl.CostEstimate(flops=10**7, bytes_accessed=8 * 10**6, transcendentals=0),
        compiler_params=pltpu.CompilerParams(vmem_limit_bytes=16 * MIB),
    )(state)


def edge_kernel(sums, rims, above, below, edge, left, right):
    lane = lanes(SRC)
    outer = (lane < 4) | (lane >= 124)
    packed = [[jnp.zeros((SRC, 128), F) for _ in range(2)] for _ in range(2)]
    for p in range(ROWS):
        main = sums[p, :, :128].astype(F)
        side = sums[p, :, 128:].astype(F)
        if p < 8 or p >= 24:
            msg, i, e = (above, p, p) if p < 8 else (below, p - 24, p - 16)
            main = main + msg[i * SRC:(i + 1) * SRC].astype(F)
            moved = pltpu.roll(msg[8 * SRC:9 * SRC].astype(F), 124 - i * 8, 1)
            side = side + jnp.where(outer, moved, 0.0)
            edge[e, :, :128] = main.astype(BF)
            edge[e, :, 128:] = side.astype(BF)
        k, shift = p // 16, (p % 16) * 8 + 4
        here = (lane >> 3) == p % 16
        packed[0][k] = jnp.where(here, pltpu.roll(jnp.where(lane < 4, main, side), shift, 1), packed[0][k])
        packed[1][k] = jnp.where(here, pltpu.roll(jnp.where(lane >= 124, main, side), shift, 1), packed[1][k])
    for k in range(2):
        left[k * SRC:(k + 1) * SRC] = packed[0][k].astype(BF)
        right[k * SRC:(k + 1) * SRC] = packed[1][k].astype(BF)
    for c in range(0, 256, 64):
        for k, msg, first in ((0, above, 1), (1, below, 28)):
            out = rims[k * 256 + c:k * 256 + c + 64].astype(F)
            for j in range(3):
                p = first + j
                x = msg[LAT_STATE + j * 256 + c:LAT_STATE + j * 256 + c + 64].astype(F)
                out = jnp.where((lanes(64) >> 3) == p % 16, pltpu.roll(x, (p % 16) * 8 + 4, 1), out)
            at = LON_STATE + k * 256 + c
            left[at:at + 64] = out.astype(BF)
            right[at:at + 64] = out.astype(BF)


def edge_sums(sums, rims, above, below):
    shape = jax.ShapeDtypeStruct
    return pl.pallas_call(
        edge_kernel, name="edge_sums",
        out_shape=(shape((16, SRC, 256), BF), shape((LON_MSG, 128), BF), shape((LON_MSG, 128), BF)),
        compiler_params=pltpu.CompilerParams(vmem_limit_bytes=16 * MIB),
    )(sums, rims, above, below)


def prepare_kernel(base, w_in, w_up, w_down, b1, toe, wi, w1, w2, b1c):
    wi[...] = w_in[...].astype(F).T.astype(BF)
    w1[...] = w_up[...].T
    w2[...] = w_down[...].T
    b1c[...] = b1[...].T

    def step(i, _):
        rows = base[pl.ds(pl.multiple_of(i * 8, 8), 8), :]
        for k in range(8):
            parts = []
            for ln in range(2):
                b = jnp.broadcast_to(rows[k:k + 1, ln * 128:(ln + 1) * 128], (24, 128))
                parts.append(pltpu.roll(b, 0, 1, stride=1, stride_axis=0))
            y = jnp.concatenate(parts, 1).astype(BF)
            toe[i * 4 + k // 2, (k % 2) * 24:(k % 2) * 24 + 24, :] = y[:, :224]
        return 0

    lax.fori_loop(0, 32, step, 0)


def prepare(dw_weight, w_in, w_up, w_down, up_bias):
    base = jnp.pad(jnp.swapaxes(dw_weight, 1, 2), ((0, 0), (0, 1), (1, 24))).reshape(256, 256)
    shape = jax.ShapeDtypeStruct
    return pl.pallas_call(
        prepare_kernel, name="prepare",
        out_shape=(shape((128, 48, 224), BF), shape((256, SRC), BF), shape((1024, 256), BF), shape((256, 1024), BF), shape((128, 8), F)),
        cost_estimate=pl.CostEstimate(flops=10**7, bytes_accessed=8 * 10**6, transcendentals=0),
        compiler_params=pltpu.CompilerParams(vmem_limit_bytes=24 * MIB),
    )(base, jnp.pad(w_in, ((0, SRC - 65), (0, 0))), w_up, w_down, up_bias.reshape(8, 128))


def shift_matrix():
    lane = lax.broadcasted_iota(jnp.int32, (256, 768), 0)
    out = lax.broadcasted_iota(jnp.int32, (256, 768), 1)
    col = jnp.where(lane < 132, lane, jnp.where(lane >= 252, lane - 256, -1000))
    k = out // 128
    d = jnp.where(k < 3, k - 3, k - 2)
    return jnp.where(col == out % 128 + d, 1.0, 0.0).astype(BF)


def block_kernel(dwb, gain, nbias, db, ls, sums, edge, above, below, rows, left, right, toe, wi, w1, b1, w2, out,
                 mixed, native, xs, filt, xbuf, obuf, smat):
    smat[...] = shift_matrix()
    lane = lanes(SRC)
    low, high = lane < 4, lane >= 124
    wide = lanes(256)
    outer = (wide < 4) | (wide >= 124)

    def encode(p, main, side, state):
        k, shift = p // 16, (124 - (p % 16) * 8) % 128
        at = pl.ds(pl.multiple_of(k * SRC, SRC), SRC)
        a = pltpu.roll(left[at].astype(F), shift, 1)
        b = pltpu.roll(right[at].astype(F), shift, 1)
        main = main.astype(F) + jnp.where(low, a, jnp.where(high, b, 0.0))
        side = side.astype(F) + jnp.where(high, a, jnp.where(low, b, 0.0))
        src = jnp.concatenate([main, side], 1).astype(BF)
        both = jnp.dot(wi[...], src, preferred_element_type=F)
        at = pl.ds(pl.multiple_of(LON_STATE + k * 256, 32), 256)
        rim = jnp.where((wide & 7) < 4, left[at].astype(F), right[at].astype(F))
        rim = jnp.where(outer, pltpu.roll(rim, shift, 1), 0.0)
        mixed[p, :, :128] = (both[:, :128] + state.astype(F)).astype(BF)
        mixed[p, :, 128:] = (both[:, 128:] + rim).astype(BF)

    def halo_row(j, _):
        at = pl.ds(pl.multiple_of(LAT_STATE + j * 256, 16), 256)
        encode(1 + j, edge[1 + j, :, :128], edge[1 + j, :, 128:], above[at])
        encode(28 + j, edge[12 + j, :, :128], edge[12 + j, :, 128:], below[at])
        return 0

    def edge_row(j, _):
        encode(4 + j, edge[4 + j, :, :128], edge[4 + j, :, 128:], rows[j])
        encode(24 + j, edge[8 + j, :, :128], edge[8 + j, :, 128:], rows[20 + j])
        return 0

    def inner_row(j, _):
        encode(8 + j, sums[8 + j, :, :128], sums[8 + j, :, 128:], rows[4 + j])
        return 0

    mixed[0] = jnp.zeros((256, 256), BF)
    mixed[31] = jnp.zeros((256, 256), BF)
    lax.fori_loop(0, 3, halo_row, 0)
    lax.fori_loop(0, 4, edge_row, 0)
    lax.fori_loop(0, 16, inner_row, 0)

    def filt_step(i, s1):
        c0 = pl.multiple_of(i * CB, CB)
        turned = jnp.swapaxes(mixed[:, pl.ds(c0, CB), :].astype(F), 0, 1).astype(BF)
        native[pl.ds(c0, CB)] = turned[:, :, :128]
        m = turned.reshape(CB * ROWS, 256)
        for j in range(3):
            z = jnp.dot(m, smat[:, j * 256:(j + 1) * 256], preferred_element_type=F).astype(BF)
            for half in range(2):
                k = 2 * j + half
                v = k if k < 3 else k + 1
                zz = z[:, half * 128:(half + 1) * 128]
                for c in range(CB):
                    xs[c // 2, v * 32:(v + 1) * 32, (c % 2) * 128:(c % 2) * 128 + 128] = zz[c * 32:(c + 1) * 32]
        for c in range(CB):
            xs[c // 2, 96:128, (c % 2) * 128:(c % 2) * 128 + 128] = m[c * 32:(c + 1) * 32, :128]
        for k in range(CB // 2):
            o = jnp.dot(toe[i * (CB // 2) + k], xs[k], preferred_element_type=F)
            a = o[:24, :128] + dwb[c0 + 2 * k]
            b = o[24:, 128:] + dwb[c0 + 2 * k + 1]
            filt[c0 + 2 * k] = a
            filt[c0 + 2 * k + 1] = b
            s1 = s1 + (a + b)
        return s1

    s1 = lax.fori_loop(0, 256 // CB, filt_step, jnp.zeros((24, 128), F))
    mean = s1 * (1.0 / 256)

    def var_step(i, s2):
        for k in range(16):
            a = filt[i * 16 + k] - mean
            s2 = s2 + a * a
        return s2

    s2 = lax.fori_loop(0, 16, var_step, jnp.zeros((24, 128), F))
    rstd = lax.rsqrt(s2 * (1.0 / 256) + 1e-6)

    def norm_step(i, _):
        c0 = pl.multiple_of(i * 16, 16)
        ys = [((filt[c0 + k] - mean) * rstd) * gain[c0 + k] + nbias[c0 + k] for k in range(16)]
        xbuf[:, pl.ds(c0, 16), :] = jnp.swapaxes(jnp.stack(ys, 0), 0, 1).astype(BF)
        return 0

    lax.fori_loop(0, 16, norm_step, 0)

    def mlp_step(i, _):
        x = jnp.concatenate([xbuf[i * RB + k] for k in range(RB)], 1)
        h = jnp.dot(w1[...], x, preferred_element_type=F)
        gs = []
        for k in range(8):
            hk = h[k * 128:(k + 1) * 128] + b1[:, k:k + 1]
            gs.append(((0.5 * hk) * (1.0 + lax.erf(hk * 0.7071067811865476))).astype(BF))
        o = jnp.dot(w2[...], jnp.concatenate(gs, 0), preferred_element_type=F)
        for k in range(RB):
            obuf[i * RB + k] = o[:, k * 128:(k + 1) * 128]
        return 0

    lax.fori_loop(0, 24 // RB, mlp_step, 0)

    def out_step(i, _):
        c0 = pl.multiple_of(i * 16, 16)
        o = jnp.swapaxes(obuf[:, pl.ds(c0, 16), :], 0, 1)
        m = native[pl.ds(c0, 16)].astype(F)
        for k in range(16):
            out[c0 + k] = (m[k, 4:28] + (o[k] + db[c0 + k]) * ls[c0 + k]).astype(BF)
        return 0

    lax.fori_loop(0, 16, out_step, 0)


def block(arrays, vectors):
    S = pl.BlockSpec(memory_space=pltpu.SMEM)
    V = pl.BlockSpec(memory_space=pltpu.VMEM)
    return pl.pallas_call(
        block_kernel, name="block", out_shape=jax.ShapeDtypeStruct((256, 24, 128), BF),
        in_specs=[S] * len(vectors) + [V] * len(arrays), out_specs=V,
        scratch_shapes=[
            pltpu.VMEM((ROWS, 256, 256), BF), pltpu.VMEM((256, ROWS, 128), BF), pltpu.VMEM((CB // 2, 224, 256), BF),
            pltpu.VMEM((256, 24, 128), F), pltpu.VMEM((24, 256, 128), BF), pltpu.VMEM((24, 256, 128), F),
            pltpu.VMEM((256, 768), BF),
        ],
        compiler_params=pltpu.CompilerParams(vmem_limit_bytes=48 * MIB),
    )(*vectors, *arrays)


def exchange(to_lower, to_upper, axis, wrap):
    size = lax.axis_size(axis)
    up = [(i, (i + 1) % size) for i in range(size if wrap else size - 1)]
    down = [(j, i) for i, j in up]
    return lax.ppermute(to_upper, axis, up), lax.ppermute(to_lower, axis, down)


def local(state, obs_values, obs_offsets, obs_cell, obs_count, w_in, dw_weight, dw_bias, norm_gain, norm_bias,
          w_up, up_bias, w_down, down_bias, layer_scale):
    row_base = (lax.axis_index("lat") * state.shape[1]).astype(jnp.int32).reshape(1)
    sums, up, down = observation_sums(obs_values, obs_offsets, obs_cell, obs_count, row_base, state)
    above, below = exchange(up, down, "lat", False)
    state_later, _ = lax.optimization_barrier((state, sums))
    rows, rims = state_rows(state_later)
    edge, left, right = edge_sums(sums, rims, above, below)
    from_left, from_right = exchange(left, right, "lon", True)
    dw_later, w_up_later, w_down_later, _ = lax.optimization_barrier((dw_weight, w_up, w_down, edge))
    toe, wi, w1, w2, b1 = prepare(dw_later, w_in, w_up_later, w_down_later, up_bias)
    return block(
        (sums, edge, above, below, rows, from_left, from_right, toe, wi, w1, b1, w2),
        (dw_bias, norm_gain, norm_bias, down_bias, layer_scale),
    )


def solution(mesh):
    return jax.shard_map(
        local,
        mesh=mesh,
        in_specs=(
            P(None, "lat", "lon"),
            P(None, ("lat", "lon")),
            P(None, ("lat", "lon")),
            P(("lat", "lon")),
            P(("lat", "lon")),
            P(),
            P(),
            P(),
            P(),
            P(),
            P(),
            P(),
            P(),
            P(),
            P(),
        ),
        out_specs=P(None, "lat", "lon"),
        check_vma=False,
    )
```

time: 153 us -> 75.4 us (0.49)
  the two profiles are of different devices: /device:TPU:23 before, /device:TPU:1 now
where the time goes in v2:
time: 75.4 us; the launch traced here: 75 us
  Pallas kernels  37.7 us (50%)
  starting transfers between devices  15.1 us (20%)
  local copies, waits for them, and re-layouts  12.4 us (16%)
  waiting for transfers between devices  9.07 us (12%)
  between operations  0.84 us (1%)
    pallas_call x1, Pallas kernels, block(): pl.pallas_call(block_kernel, name='block', out_shape=jax.ShapeDtypeStruct...  29.2 us
    unnamed x40, local copies, waits for them, and re-layouts  9.95 us
    ppermute x2, starting transfers between devices, exchange(): lax.ppermute(to_lower, axis, down)  7.92 us
    ppermute x2, waiting for transfers between devices, exchange(): lax.ppermute(to_lower, axis, down)  7.73 us
    ppermute x2, starting transfers between devices, exchange(): lax.ppermute(to_upper, axis, up)  7.15 us
    pallas_call x1, Pallas kernels, prepare(): pl.pallas_call(prepare_kernel, name='prepare', out_shape=(shape((128, 48,...  3.45 us
    pallas_call x1, Pallas kernels, edge_sums(): pl.pallas_call(edge_kernel, name='edge_sums', out_shape=(shape((16, SRC,...  2.19 us
    pallas_call x1, Pallas kernels, observation_sums(): pl.pallas_call(sums_kernel, name='observation_sums', out_shape=(shape((RO...  1.6 us
  transfers between devices with their start and end apart: 4, of which 2 were waited for; matrix products, arithmetic and copies ran while one was open for 3% of the time, Pallas kernels for 6%

profile of v2, /device:TPU:1, one launch (start us, length us, event | category | flops | bytes accessed | tf_op | source)
XLA Modules:
  0.0 75.0 jit_solution(15082870241443339261)
XLA Ops:
  0.7 0.0 copy-start
  0.7 1.4 %copy-done = bf16[256,24,128]{2,1,0:T(8,128)(2,1)S(1)} copy-done((bf16[256,24,128]{2,1,0:T(8,128)(2,1)S(1)}, bf16[256,24,128]{2,1,0:T(8,128)(2,1)}, u32[]{:S(2)}) %copy-start) | copy-done | bytes 1572888
  2.1 0.0 copy-start.8
  2.1 0.9 %copy-done.8 = bf16[64,2048]{1,0:T(8,128)(2,1)S(1)} copy-done((bf16[64,2048]{1,0:T(8,128)(2,1)S(1)}, bf16[64,2048]{1,0:T(8,128)(2,1)}, u32[]{:S(2)}) %copy-start.8) | copy-done | bytes 262168
  3.0 0.0 copy-start.10
  3.0 0.7 copy-done.10
  3.7 0.0 copy-start.11
  3.7 0.7 copy-done.11
  4.4 1.6 %observation_sums.1 = (bf16[32,80,256]{2,1,0:T(8,128)(2,1)S(1)}, bf16[1488,128]{1,0:T(8,128)(2,1)S(1)}, bf16[1488,128]{1,0:T(8,128)(2,1)S(1)}) custom-call(s32[1]{0:T(128)S(6)} %copy.21.count, s32[1]{0:T(128)} %bitcast.row_base, bf16[64,2048]{1,0:T(8,128)(2,1)S(1)} %copy-done.8, f32[2,2048]{1,0:T(2,128)S(1)} %copy-done.10, s32[1,2048]{1,0:T(1,128)S(1)} %bitcast.7, ...), custom_call_target="tpu_custom_call" | custom-call | tf_op jit(solution)/shard_map/observation_sums/pallas_call | solution.py:87
  6.0 4.5 %collective-permute-start = (bf16[1488,128]{1,0:T(8,128)(2,1)S(1)}, bf16[1488,128]{1,0:T(8,128)(2,1)S(1)}, u32[]{:S(2)}, u32[]{:S(2)}) collective-permute-start(bf16[1488,128]{1,0:T(8,128)(2,1)S(1)} %get-tuple-element.25), channel_id=1, source_target_pairs={{0,16},{16,32},{32,48},{48,64},{64,80},{80,96},{96,112},{112,128},... | collective-permute-start | bytes 1142792 | tf_op jit(solution)/shard_map/ppermute | solution.py:336
  10.6 2.0 %collective-permute-start.1 = (bf16[1488,128]{1,0:T(8,128)(2,1)S(1)}, bf16[1488,128]{1,0:T(8,128)(2,1)S(1)}, u32[]{:S(2)}, u32[]{:S(2)}) collective-permute-start(bf16[1488,128]{1,0:T(8,128)(2,1)S(1)} %get-tuple-element.26), channel_id=1, source_target_pairs={{16,0},{32,16},{48,32},{64,48},{80,64},{96,80},{112,96},{128,112},... | collective-permute-start | bytes 1142792 | tf_op jit(solution)/shard_map/ppermute | solution.py:336
  12.5 0.0 copy-start.19
  12.5 0.0 copy-start.18
  12.5 1.2 %state_rows.1 = (bf16[24,256,128]{2,1,0:T(8,128)(2,1)S(1)}, bf16[512,128]{1,0:T(8,128)(2,1)S(1)}) custom-call(bf16[256,24,128]{2,1,0:T(8,128)(2,1)S(1)} %copy-done), custom_call_target="tpu_custom_call" | custom-call | flops 10000000 | bytes 8000000 | tf_op jit(solution)/shard_map/state_rows/pallas_call | solution.py:115
  13.8 1.3 %collective-permute-done.above = bf16[1488,128]{1,0:T(8,128)(2,1)S(1)} collective-permute-done((bf16[1488,128]{1,0:T(8,128)(2,1)S(1)}, bf16[1488,128]{1,0:T(8,128)(2,1)S(1)}, u32[]{:S(2)}, u32[]{:S(2)}) %collective-permute-start) | collective-permute-done | bytes 380960 | tf_op jit(solution)/shard_map/ppermute | solution.py:336
  15.1 7.7 %collective-permute-done.1.below = bf16[1488,128]{1,0:T(8,128)(2,1)S(1)} collective-permute-done((bf16[1488,128]{1,0:T(8,128)(2,1)S(1)}, bf16[1488,128]{1,0:T(8,128)(2,1)S(1)}, u32[]{:S(2)}, u32[]{:S(2)}) %collective-permute-start.1) | collective-permute-done | bytes 380960 | tf_op jit(solution)/shard_map/ppermute | solution.py:336
  22.8 0.0 copy-start.12
  22.8 2.2 %edge_sums.1 = (bf16[16,80,256]{2,1,0:T(8,128)(2,1)S(1)}, bf16[672,128]{1,0:T(8,128)(2,1)}, bf16[672,128]{1,0:T(8,128)(2,1)}) custom-call(bf16[32,80,256]{2,1,0:T(8,128)(2,1)S(1)} %get-tuple-element.22.sums, bf16[512,128]{1,0:T(8,128)(2,1)S(1)} %get-tuple-element.24.rims, bf16[1488,128]{1,0:T(8,128)(2,1)S(1)} %collective-permute-done.above, ...), custom_call_target="tpu_custom_call" | custom-call | tf_op jit(solution)/shard_map/edge_sums/pallas_call | solution.py:157
  25.0 0.0 copy-start.2
  25.0 0.7 copy-done.2
  25.8 0.0 copy-start.4
  25.8 0.8 %copy-done.4 = bf16[16,80,256]{2,1,0:T(8,128)(2,1)} copy-done((bf16[16,80,256]{2,1,0:T(8,128)(2,1)}, bf16[16,80,256]{2,1,0:T(8,128)(2,1)S(1)}, u32[]{:S(2)}) %copy-start.4) | copy-done | bytes 655384
  26.6 0.0 copy-start.13
  26.6 0.0 copy-start.14
  26.6 0.0 copy-start.15
  26.6 0.0 copy-start.16
  26.6 0.0 copy-start.17
  26.6 2.6 %collective-permute-start.2 = (bf16[672,128]{1,0:T(8,128)(2,1)}, bf16[672,128]{1,0:T(8,128)(2,1)}, u32[]{:S(2)}, u32[]{:S(2)}) collective-permute-start(bf16[672,128]{1,0:T(8,128)(2,1)} %get-tuple-element.29), channel_id=1, source_target_pairs={{0,1},{1,2},{2,3},{3,4},{4,5},{5,6},{6,7},{7,8},{8,9},{9,10},{10,1... | collective-permute-start | bytes 516104 | tf_op jit(solution)/shard_map/ppermute | solution.py:336
  29.3 6.0 %collective-permute-start.3 = (bf16[672,128]{1,0:T(8,128)(2,1)}, bf16[672,128]{1,0:T(8,128)(2,1)}, u32[]{:S(2)}, u32[]{:S(2)}) collective-permute-start(bf16[672,128]{1,0:T(8,128)(2,1)} %get-tuple-element.30), channel_id=1, source_target_pairs={{1,0},{2,1},{3,2},{4,3},{5,4},{6,5},{7,6},{8,7},{9,8},{10,9},{11,1... | collective-permute-start | bytes 516104 | tf_op jit(solution)/shard_map/ppermute | solution.py:336
  35.2 0.0 copy-done.19
  35.2 0.6 pad.9.w_in
  35.8 0.0 copy-done.18
  35.9 0.7 pad.8
  36.6 1.1 %copy.18.base = f32[256,256]{1,0:T(8,128)S(1)} copy(f32[256,256]{0,1:T(8,128)} %bitcast.9) | data formatting | bytes 524288 | tf_op jit(solution)/shard_map/reshape | solution.py:185
  37.7 0.0 copy-start.3
  37.7 0.0 copy-start.5
  37.7 0.0 copy-done.12
  37.7 0.0 copy-start.6
  37.7 1.1 %copy-done.6 = bf16[256,1024]{1,0:T(8,128)(2,1)S(1)} copy-done((bf16[256,1024]{1,0:T(8,128)(2,1)S(1)}, bf16[256,1024]{1,0:T(8,128)(2,1)}, u32[]{:S(2)}) %copy-start.6) | copy-done | bytes 524312
  38.8 0.0 copy-start.7
  38.8 1.0 %copy-done.7 = bf16[1024,256]{1,0:T(8,128)(2,1)S(1)} copy-done((bf16[1024,256]{1,0:T(8,128)(2,1)S(1)}, bf16[1024,256]{1,0:T(8,128)(2,1)}, u32[]{:S(2)}) %copy-start.7) | copy-done | bytes 524312
  39.9 0.0 copy-start.9
  39.9 0.8 %copy-done.9 = bf16[80,256]{1,0:T(8,128)(2,1)S(1)} copy-done((bf16[80,256]{1,0:T(8,128)(2,1)S(1)}, bf16[80,256]{1,0:T(8,128)(2,1)}, u32[]{:S(2)}) %copy-start.9) | copy-done | bytes 40984
  40.7 3.5 %prepare.1 = (bf16[128,48,224]{2,1,0:T(8,128)(2,1)S(1)}, bf16[256,80]{1,0:T(8,128)(2,1)S(1)}, bf16[1024,256]{1,0:T(8,128)(2,1)S(1)}, bf16[256,1024]{1,0:T(8,128)(2,1)S(1)}, f32[128,8]{1,0:T(8,128)S(1)}) custom-call(f32[256,256]{1,0:T(8,128)S(1)} %copy.18.base, bf16[80,256]{1,0:T(8,128)(2,1)S(1)} %copy-done.9, bf16[256,1024]{1,0:T(8,128)(2,1)S(1)} %copy-done.6, ...), custom_call_target="tpu_custom_call" | custom-call | flops 10000000 | bytes 8000000 | tf_op jit(solution)/shard_map/prepare/pallas_call | solution.py:187
  44.1 0.0 copy-start.1
  44.1 1.6 %copy-done.1 = bf16[128,48,224]{2,1,0:T(8,128)(2,1)} copy-done((bf16[128,48,224]{2,1,0:T(8,128)(2,1)}, bf16[128,48,224]{2,1,0:T(8,128)(2,1)S(1)}, u32[]{:S(2)}) %copy-start.1) | copy-done | bytes 2752536
  45.7 0.0 collective-permute-done.2.left
  45.8 0.0 collective-permute-done.3.right
  45.8 0.0 copy-done.13
  45.8 0.0 copy-done.14
  45.8 0.0 copy-done.15
  45.8 0.0 copy-done.16
  45.8 0.0 copy-done.17
  45.8 0.0 copy-done.3
  45.8 0.0 copy-done.5
  45.8 29.2 %block.1 = bf16[256,24,128]{2,1,0:T(8,128)(2,1)} custom-call(f32[256]{0:T(256)S(1)} %copy-done.13, f32[256]{0:T(256)S(1)} %copy-done.14, f32[256]{0:T(256)S(1)} %copy-done.15, f32[256]{0:T(256)S(1)} %copy-done.16, f32[256]{0:T(256)S(1)} %copy-done.17, bf16[32,80,256]{2,1,0:T(8,128)(2,1)S(1)} %get-tuple-element.22.sums, bf16[16,80,256]{2,1,0:T(8,128)(2,1)S(1)} %copy-done.5, ...), custom_call_target="tpu_custom_call" | custom-call | tf_op jit(solution)/shard_map/block/pallas_call | solution.py:320
  (1 shorter events, 0.0 us)
Async XLA Ops:
  0.7 1.4 %copy-start = (bf16[256,24,128]{2,1,0:T(8,128)(2,1)S(1)}, bf16[256,24,128]{2,1,0:T(8,128)(2,1)}, u32[]{:S(2)}) copy-start(bf16[256,24,128]{2,1,0:T(8,128)(2,1)} %state.2) | copy-start | bytes 4718596
  2.1 0.9 %copy-start.8 = (bf16[64,2048]{1,0:T(8,128)(2,1)S(1)}, bf16[64,2048]{1,0:T(8,128)(2,1)}, u32[]{:S(2)}) copy-start(bf16[64,2048]{1,0:T(8,128)(2,1)} %vals.1) | copy-start | bytes 786436
  3.0 0.7 copy-start.10
  3.7 0.7 copy-start.11
  6.0 9.1 %collective-permute-start = (bf16[1488,128]{1,0:T(8,128)(2,1)S(1)}, bf16[1488,128]{1,0:T(8,128)(2,1)S(1)}, u32[]{:S(2)}, u32[]{:S(2)}) collective-permute-start(bf16[1488,128]{1,0:T(8,128)(2,1)S(1)} %get-tuple-element.25), channel_id=1, source_target_pairs={{0,16},{16,32},{32,48},{48,64},{64,80},{80,96},{96,112},{112,128},... | collective-permute-start | bytes 1142792 | tf_op jit(solution)/shard_map/ppermute | solution.py:336
  10.6 12.3 %collective-permute-start.1 = (bf16[1488,128]{1,0:T(8,128)(2,1)S(1)}, bf16[1488,128]{1,0:T(8,128)(2,1)S(1)}, u32[]{:S(2)}, u32[]{:S(2)}) collective-permute-start(bf16[1488,128]{1,0:T(8,128)(2,1)S(1)} %get-tuple-element.26), channel_id=1, source_target_pairs={{16,0},{32,16},{48,32},{64,48},{80,64},{96,80},{112,96},{128,112},... | collective-permute-start | bytes 1142792 | tf_op jit(solution)/shard_map/ppermute | solution.py:336
  12.5 22.7 %copy-start.19 = (bf16[65,256]{1,0:T(8,128)(2,1)S(1)}, bf16[65,256]{1,0:T(8,128)(2,1)}, u32[]{:S(2)}) copy-start(bf16[65,256]{1,0:T(8,128)(2,1)} %param.20) | copy-start | bytes 99844
  12.5 23.3 %copy-start.18 = (f32[256,7,7]{0,2,1:T(8,128)S(1)}, f32[256,7,7]{0,2,1:T(8,128)}, u32[]{:S(2)}) copy-start(f32[256,7,7]{0,2,1:T(8,128)} %param.21) | copy-start | bytes 150532
  22.8 14.9 %copy-start.12 = (f32[1024]{0:T(1024)S(1)}, f32[1024]{0:T(1024)}, u32[]{:S(2)}) copy-start(f32[1024]{0:T(1024)} %param.26) | copy-start | bytes 12292
  25.0 0.7 copy-start.2
  25.8 0.8 %copy-start.4 = (bf16[16,80,256]{2,1,0:T(8,128)(2,1)}, bf16[16,80,256]{2,1,0:T(8,128)(2,1)S(1)}, u32[]{:S(2)}) copy-start(bf16[16,80,256]{2,1,0:T(8,128)(2,1)S(1)} %get-tuple-element.27.edge) | copy-start | bytes 1966084
  26.6 19.1 %copy-start.13 = (f32[256]{0:T(256)S(1)}, f32[256]{0:T(256)}, u32[]{:S(2)}) copy-start(f32[256]{0:T(256)} %dwb.1) | copy-start | bytes 3076
  26.6 19.1 %copy-start.14 = (f32[256]{0:T(256)S(1)}, f32[256]{0:T(256)}, u32[]{:S(2)}) copy-start(f32[256]{0:T(256)} %gain.1) | copy-start | bytes 3076
  26.6 19.2 %copy-start.15 = (f32[256]{0:T(256)S(1)}, f32[256]{0:T(256)}, u32[]{:S(2)}) copy-start(f32[256]{0:T(256)} %nbias.1) | copy-start | bytes 3076
  26.6 19.2 %copy-start.16 = (f32[256]{0:T(256)S(1)}, f32[256]{0:T(256)}, u32[]{:S(2)}) copy-start(f32[256]{0:T(256)} %db.1) | copy-start | bytes 3076
  26.6 19.2 %copy-start.17 = (f32[256]{0:T(256)S(1)}, f32[256]{0:T(256)}, u32[]{:S(2)}) copy-start(f32[256]{0:T(256)} %ls.1) | copy-start | bytes 3076
  26.6 19.1 %collective-permute-start.2 = (bf16[672,128]{1,0:T(8,128)(2,1)}, bf16[672,128]{1,0:T(8,128)(2,1)}, u32[]{:S(2)}, u32[]{:S(2)}) collective-permute-start(bf16[672,128]{1,0:T(8,128)(2,1)} %get-tuple-element.29), channel_id=1, source_target_pairs={{0,1},{1,2},{2,3},{3,4},{4,5},{5,6},{6,7},{7,8},{8,9},{9,10},{10,1... | collective-permute-start | bytes 516104 | tf_op jit(solution)/shard_map/ppermute | solution.py:336
  29.3 16.5 %collective-permute-start.3 = (bf16[672,128]{1,0:T(8,128)(2,1)}, bf16[672,128]{1,0:T(8,128)(2,1)}, u32[]{:S(2)}, u32[]{:S(2)}) collective-permute-start(bf16[672,128]{1,0:T(8,128)(2,1)} %get-tuple-element.30), channel_id=1, source_target_pairs={{1,0},{2,1},{3,2},{4,3},{5,4},{6,5},{7,6},{8,7},{9,8},{10,9},{11,1... | collective-permute-start | bytes 516104 | tf_op jit(solution)/shard_map/ppermute | solution.py:336
  37.7 8.1 %copy-start.3 = (bf16[1488,128]{1,0:T(8,128)(2,1)S(1)}, bf16[1488,128]{1,0:T(8,128)(2,1)}, u32[]{:S(2)}) copy-start(bf16[1488,128]{1,0:T(8,128)(2,1)} %copy-done.2) | copy-start | bytes 1142788
  37.7 8.1 %copy-start.5 = (bf16[16,80,256]{2,1,0:T(8,128)(2,1)S(1)}, bf16[16,80,256]{2,1,0:T(8,128)(2,1)}, u32[]{:S(2)}) copy-start(bf16[16,80,256]{2,1,0:T(8,128)(2,1)} %copy-done.4) | copy-start | bytes 1966084
  37.7 1.1 %copy-start.6 = (bf16[256,1024]{1,0:T(8,128)(2,1)S(1)}, bf16[256,1024]{1,0:T(8,128)(2,1)}, u32[]{:S(2)}) copy-start(bf16[256,1024]{1,0:T(8,128)(2,1)} %w_up) | copy-start | bytes 1572868
  38.8 1.0 %copy-start.7 = (bf16[1024,256]{1,0:T(8,128)(2,1)S(1)}, bf16[1024,256]{1,0:T(8,128)(2,1)}, u32[]{:S(2)}) copy-start(bf16[1024,256]{1,0:T(8,128)(2,1)} %w_down) | copy-start | bytes 1572868
  39.9 0.8 %copy-start.9 = (bf16[80,256]{1,0:T(8,128)(2,1)S(1)}, bf16[80,256]{1,0:T(8,128)(2,1)}, u32[]{:S(2)}) copy-start(bf16[80,256]{1,0:T(8,128)(2,1)} %pad.9.w_in) | copy-start | bytes 122884
  44.1 1.6 %copy-start.1 = (bf16[128,48,224]{2,1,0:T(8,128)(2,1)}, bf16[128,48,224]{2,1,0:T(8,128)(2,1)S(1)}, u32[]{:S(2)}) copy-start(bf16[128,48,224]{2,1,0:T(8,128)(2,1)S(1)} %get-tuple-element.34.toe) | copy-start | bytes 8257540
